TPU v7x, 128 devices: a whole 4x4x4 slice. The times are simulated.
128 devices in a mesh: group: 2 (over core), blk: 64 (over z, y, x).
Axes of the slice: x: 4, y: 4, z: 4, core: 2. Of those that a mesh axis runs over, the one named last changes fastest.
Arguments:
- field: float32 [2, 64, 5, 32, 512], P('group', 'blk'), may hold values from -6 to 6
- source: float32 [2, 64, 5, 32, 512], P('group', 'blk'), may hold values from -6 to 6
- block_inverse: float32 [2, 64, 5, 5, 32, 512], P('group', 'blk'), may hold values from -0.05 to 0.14, as said below
- coupling: float32 [2, 64, 4, 32, 512], P('group', 'blk'), may hold values from 0.3 to 1.2
- donor_base: int32 [2, 64, 64, 256], P('group', 'blk'), may hold values from 0 to 15870
- donor_weight: float32 [2, 64, 4, 64, 256], P('group', 'blk'), may hold values from 0 to 1, as said below
- receiver_cell: int32 [2, 64, 64, 256], P('group', 'blk'), may hold values from 0 to 16384, as said below
Outputs:
- field_out: float32 [2, 64, 5, 32, 512], P('group', 'blk')
Inputs may be any that keep to these rules, and one draw needn't show every extreme that they name: `block_inverse`: the entries of a block diagonal lie in 0.06 to 0.14; other entries are at most 0.05 in magnitude. `donor_weight`: the four weights of a slot are positive and sum to one. `receiver_cell`: within one block all entries below 16384 are distinct cells; for each donor block the used slots come first and the rest hold 16384; in every block some donor block fills all 256 slots.
All inputs are finite; a program needn't handle non-finite values.
Results may differ from a plain program's by a relative error of at most 0.0003.
Values sent between devices are 32-bit elements; how exact they have to be, the bound alone decides.
A program may use at most 128 MiB of HBM per device.

v0:
```python
from functools import partial

import jax
import jax.numpy as jnp
from jax import lax
from jax.sharding import PartitionSpec as P

ITERS = 4


upwind_offsets = (-3, -2, -1, 0, 1, 2)
upwind_weights = (-2.0 / 60.0, 15.0 / 60.0, -60.0 / 60.0, 20.0 / 60.0, 30.0 / 60.0, -3.0 / 60.0)


def partner(shard, axis, stride):
    return lax.ppermute(shard, axis, [(i, i ^ 1 << stride) for i in range(lax.axis_size(axis))])


def padded_2(block, sides, width):
    for axis, dim in sides:
        count = lax.axis_size(axis)
        forward = [(i, i + 1) for i in range(count - 1)]
        backward = [(target, source) for source, target in forward]
        low = lax.ppermute(
            lax.slice_in_dim(block, block.shape[dim] - width, None, axis=dim), axis, forward
        )
        high = lax.ppermute(lax.slice_in_dim(block, 0, width, axis=dim), axis, backward)
        block = jnp.concatenate([low, block, high], axis=dim)
    return block


def window(padded, shift_j, shift_k, row_count, column_count):
    return padded[
        :, 3 + shift_j : 3 + shift_j + row_count, 3 + shift_k : 3 + shift_k + column_count
    ]


def near_half(padded, solution, forcing, inverse, coupling, update_mask):
    row_count, column_count = (solution.shape[1], solution.shape[2])
    gathered = coupling[0] * window(padded, -1, 0, row_count, column_count)
    gathered = gathered + coupling[1] * window(padded, 1, 0, row_count, column_count)
    gathered = gathered + coupling[2] * window(padded, 0, -1, row_count, column_count)
    gathered = gathered + coupling[3] * window(padded, 0, 1, row_count, column_count)
    total = forcing + gathered
    updated = jnp.sum(inverse * total[None], axis=1)
    return jnp.where(update_mask[None], updated, solution)


def off_section(padded, solution, forcing, inverse, coupling, update_mask):
    row_count, column_count = (solution.shape[1], solution.shape[2])
    along_j = jnp.zeros_like(solution)
    along_k = jnp.zeros_like(solution)
    for offset, weight in zip(upwind_offsets, upwind_weights):
        along_j = along_j + weight * window(padded, offset, 0, row_count, column_count)
        along_k = along_k + weight * window(padded, 0, offset, row_count, column_count)
    residual_term = forcing - coupling[0] * along_j - coupling[1] * along_k
    updated = solution + jnp.sum(inverse * residual_term[None], axis=1)
    return jnp.where(update_mask[None], updated, solution)


def interpolate(flat_state, row_bases, weights, column_count):
    cell_count = flat_state.shape[1]
    width = flat_state.shape[0]
    cell_major = jnp.pad(flat_state.T, ((0, column_count + 1), (0, 0)))
    corner_table = jnp.concatenate(
        [
            cell_major[0:cell_count],
            cell_major[1 : cell_count + 1],
            cell_major[column_count : column_count + cell_count],
            cell_major[column_count + 1 : column_count + 1 + cell_count],
        ],
        axis=1,
    )
    picked = jnp.take(corner_table, row_bases, axis=0)
    result = jnp.zeros((row_bases.shape[0], width), jnp.float32)
    for corner in range(4):
        result = (
            result
            + weights[corner].reshape(-1)[:, None]
            * picked[:, corner * width : (corner + 1) * width]
        )
    return result.T


def on_device(field, source, block_inverse, coupling, donor_base, donor_weight, receiver_cell):
    solution = field[0, 0]
    forcing = source[0, 0]
    inverse = block_inverse[0, 0]
    factors = coupling[0, 0]
    bases = donor_base[0, 0]
    weights = donor_weight[0, 0]
    targets = receiver_cell[0, 0].reshape(-1)
    width = solution.shape[0]
    row_count = solution.shape[1]
    column_count = solution.shape[2]
    cell_count = row_count * column_count
    block_count = bases.shape[0]
    slot_count = bases.shape[1]
    slot_total = block_count * slot_count
    row_bases = bases.reshape(-1)
    slot_of_cell = (
        jnp.full((cell_count,), slot_total, jnp.int32)
        .at[targets]
        .set(jnp.arange(slot_total, dtype=jnp.int32), mode="drop")
    )
    frozen_flat = slot_of_cell < slot_total
    movable = jnp.logical_not(frozen_flat).reshape(row_count, column_count)
    parity_grid = (
        lax.broadcasted_iota(jnp.int32, (row_count, column_count), 0)
        + lax.broadcasted_iota(jnp.int32, (row_count, column_count), 1)
    ) % 2
    group_index = lax.axis_index("group")
    is_near = group_index == 0
    for iteration in range(ITERS):
        flat_state = solution.reshape(width, cell_count)
        donor_values = interpolate(flat_state, row_bases, weights, column_count).reshape(
            width, block_count, slot_count
        )
        crossed = partner(donor_values, "group", 0)
        arrived = lax.all_to_all(crossed, "blk", split_axis=1, concat_axis=1, tiled=True)
        arrived_rows = jnp.pad(arrived.reshape(width, slot_total).T, ((0, 1), (0, 0)))
        placed = jnp.take(arrived_rows, slot_of_cell, axis=0).T
        flat_state = jnp.where(frozen_flat[None], placed, flat_state)
        solution = flat_state.reshape(solution.shape)
        for parity in range(2):
            padded = padded_2(solution, (("blk", 1),), 3)
            padded = jnp.pad(padded, ((0, 0), (0, 0), (3, 3)))
            near_mask = movable & (parity_grid == parity)
            solution = lax.cond(
                is_near,
                partial(near_half, update_mask=near_mask),
                partial(off_section, update_mask=movable),
                padded,
                solution,
                forcing,
                inverse,
                factors,
            )
    return solution[None, None]


def solution(mesh):
    in_specs = (
        P("group", "blk", None, None, None),
        P("group", "blk", None, None, None),
        P("group", "blk", None, None, None, None),
        P("group", "blk", None, None, None),
        P("group", "blk", None, None),
        P("group", "blk", None, None, None),
        P("group", "blk", None, None),
    )
    out_specs = P("group", "blk", None, None, None)
    return jax.shard_map(
        on_device, mesh=mesh, in_specs=in_specs, out_specs=out_specs, check_vma=False
    )
```

profile of v0, /device:TPU:32, one launch (start us, length us, event | category | flops | bytes accessed | tf_op | source)
XLA Modules:
  0.0 1057.7 jit_solution(3801339684962984)
XLA Ops:
  2.1 5.9 copy.126
  8.1 17.2 %pad_slice_fusion.11 = (f32[16384,5]{1,0:T(8,128)}, f32[16384,5]{1,0:T(8,128)}, f32[16384,5]{1,0:T(8,128)}) fusion(f32[16384,5]{1,0:T(8,128)} %bitcast.211), kind=kLoop, calls=%fused_computation.111 | loop fusion | bytes 1310720 | tf_op jit(solution)/shard_map/slice | solution.py:68
  25.2 17.0 %pad_maximum_fusion = f32[16384,20]{1,0:T(8,128)} fusion(f32[16384,5]{1,0:T(8,128)} %get-tuple-element.626, f32[16384,5]{1,0:T(8,128)} %get-tuple-element.625, f32[16384,5]{1,0:T(8,128)} %get-tuple-element.624, f32[16384,5]{1,0:T(8,128)} %bitcast.212), kind=kLoop, calls=%fused_computation.92 | loop fusion | flops 983040 | bytes 2621440 | tf_op jit(solution)/shard_map/concatenate | solution.py:65
  42.2 58.2 %gather_fusion = f32[16384,20]{1,0:T(8,128)} fusion(f32[16384,20]{1,0:T(8,128)} %pad_maximum_fusion, s32[16384]{0:T(1024)S(1)} %fusion.18), kind=kCustom, calls=%fused_computation.clone | custom fusion | bytes 2686976 | tf_op jit(solution)/shard_map/jit(_take)/gather | solution.py:74
  106.5 60.3 %scatter_custom_fusion = s32[16384]{0:T(1024)S(1)} fusion(s32[16384]{0:T(1024)S(1)} %bitcast.283, s32[16384]{0:T(1024)S(1)} %iota.17, s32[]{:T(128)} %constant.164.clone.1), kind=kCustom, calls=%fused_computation.188 | custom fusion | bytes 65540 | tf_op jit(solution)/shard_map/scatter | solution.py:104
  168.0 11.1 %all-to-all-start = ((f32[5,64,256]{2,0,1:T(8,128)}), f32[5,64,256]{2,0,1:T(8,128)S(1)}, u32[]{:S(2)}, u32[]{:S(2)}) async-start(f32[5,64,256]{2,0,1:T(8,128)} %copy.128), calls=%async_computation | async-start | bytes 1048576 | tf_op jit(solution)/shard_map/all_to_all | solution.py:120
  179.1 12.9 %all-to-all-done = f32[5,64,256]{2,0,1:T(8,128)S(1)} async-done(((f32[5,64,256]{2,0,1:T(8,128)}), f32[5,64,256]{2,0,1:T(8,128)S(1)}, u32[]{:S(2)}, u32[]{:S(2)}) %all-to-all-start) | async-done | bytes 327712 | tf_op jit(solution)/shard_map/all_to_all | solution.py:120
  196.8 7.8 pad.52
  204.6 58.1 %gather_fusion.1 = f32[16384,5]{1,0:T(8,128)} fusion(f32[16385,5]{1,0:T(8,128)} %pad.52, s32[16384]{0:T(1024)S(1)} %fusion.19), kind=kCustom, calls=%fused_computation.1.clone | custom fusion | bytes 720896 | tf_op jit(solution)/shard_map/jit(_take)/gather | solution.py:122
  262.7 9.5 bitcast_select_fusion.3
  272.2 5.4 copy.130
  280.1 7.7 collective-permute-start.2
  289.7 7.0 conditional.8
  289.9 5.3 copy.134
  299.7 8.5 collective-permute-start.4
  316.4 17.0 %pad_slice_fusion.8 = (f32[16384,5]{1,0:T(8,128)}, f32[16384,5]{1,0:T(8,128)}, f32[16384,5]{1,0:T(8,128)}) fusion(f32[16384,5]{1,0:T(8,128)} %bitcast.215), kind=kLoop, calls=%fused_computation.108 | loop fusion | bytes 1310720 | tf_op jit(solution)/shard_map/slice | solution.py:68
  333.4 17.0 %pad_maximum_fusion.1 = f32[16384,20]{1,0:T(8,128)} fusion(f32[16384,5]{1,0:T(8,128)} %get-tuple-element.623, f32[16384,5]{1,0:T(8,128)} %get-tuple-element.622, f32[16384,5]{1,0:T(8,128)} %get-tuple-element.621, f32[16384,5]{1,0:T(8,128)} %bitcast.216), kind=kLoop, calls=%fused_computation.93 | loop fusion | flops 983040 | bytes 2621440 | tf_op jit(solution)/shard_map/concatenate | solution.py:65
  350.4 57.8 %gather_fusion.2 = f32[16384,20]{1,0:T(8,128)} fusion(f32[16384,20]{1,0:T(8,128)} %pad_maximum_fusion.1, s32[16384]{0:T(1024)S(1)} %copy-done.12), kind=kCustom, calls=%fused_computation.2.clone | custom fusion | bytes 2686976 | tf_op jit(solution)/shard_map/jit(_take)/gather | solution.py:74
  408.2 6.3 copy.136
  418.3 23.0 %all_to_all.20 = f32[5,64,256]{2,0,1:T(8,128)S(1)} all-to-all(f32[5,64,256]{2,0,1:T(8,128)S(1)} %copy.137), channel_id=1, replica_groups=mesh['group'=2,'blk'=64] {'blk'}, dimensions={1} | all-to-all | bytes 655360 | tf_op jit(solution)/shard_map/all_to_all | solution.py:120
  446.2 7.8 pad.56
  454.0 57.8 %gather_fusion.3 = f32[16384,5]{1,0:T(8,128)} fusion(f32[16385,5]{1,0:T(8,128)} %pad.56, s32[16384]{0:T(1024)S(1)} %copy-done.16), kind=kCustom, calls=%fused_computation.5.clone | custom fusion | bytes 720896 | tf_op jit(solution)/shard_map/jit(_take)/gather | solution.py:122
  511.7 9.5 bitcast_select_fusion.2
  528.9 7.7 collective-permute-start.7
  538.5 6.8 conditional.10
  548.3 8.5 collective-permute-start.9
  565.2 17.0 %pad_slice_fusion.5 = (f32[16384,5]{1,0:T(8,128)}, f32[16384,5]{1,0:T(8,128)}, f32[16384,5]{1,0:T(8,128)}) fusion(f32[16384,5]{1,0:T(8,128)} %bitcast.217), kind=kLoop, calls=%fused_computation.105 | loop fusion | bytes 1310720 | tf_op jit(solution)/shard_map/slice | solution.py:68
  582.1 17.0 %pad_maximum_fusion.2 = f32[16384,20]{1,0:T(8,128)} fusion(f32[16384,5]{1,0:T(8,128)} %get-tuple-element.620, f32[16384,5]{1,0:T(8,128)} %get-tuple-element.619, f32[16384,5]{1,0:T(8,128)} %get-tuple-element.618, f32[16384,5]{1,0:T(8,128)} %bitcast.218), kind=kLoop, calls=%fused_computation.94 | loop fusion | flops 983040 | bytes 2621440 | tf_op jit(solution)/shard_map/concatenate | solution.py:65
  599.2 57.8 %gather_fusion.4 = f32[16384,20]{1,0:T(8,128)} fusion(f32[16384,20]{1,0:T(8,128)} %pad_maximum_fusion.2, s32[16384]{0:T(1024)S(1)} %copy-done.13), kind=kCustom, calls=%fused_computation.3.clone | custom fusion | bytes 2686976 | tf_op jit(solution)/shard_map/jit(_take)/gather | solution.py:74
  656.9 6.3 copy.145
  667.1 22.6 %all_to_all.21 = f32[5,64,256]{2,0,1:T(8,128)S(1)} all-to-all(f32[5,64,256]{2,0,1:T(8,128)S(1)} %copy.146), channel_id=1, replica_groups=mesh['group'=2,'blk'=64] {'blk'}, dimensions={1} | all-to-all | bytes 655360 | tf_op jit(solution)/shard_map/all_to_all | solution.py:120
  694.6 7.8 pad.60
  702.3 57.8 %gather_fusion.5 = f32[16384,5]{1,0:T(8,128)} fusion(f32[16385,5]{1,0:T(8,128)} %pad.60, s32[16384]{0:T(1024)S(1)} %copy-done.17), kind=kCustom, calls=%fused_computation.6.clone | custom fusion | bytes 720896 | tf_op jit(solution)/shard_map/jit(_take)/gather | solution.py:122
  760.1 9.5 bitcast_select_fusion.1
  777.3 7.7 collective-permute-start.12
  786.9 7.0 conditional.12
  796.9 8.5 collective-permute-start.14
  813.6 17.0 %pad_slice_fusion.2 = (f32[16384,5]{1,0:T(8,128)}, f32[16384,5]{1,0:T(8,128)}, f32[16384,5]{1,0:T(8,128)}) fusion(f32[16384,5]{1,0:T(8,128)} %bitcast.213), kind=kLoop, calls=%fused_computation.102 | loop fusion | bytes 1310720 | tf_op jit(solution)/shard_map/slice | solution.py:68
  830.6 17.0 %pad_maximum_fusion.3 = f32[16384,20]{1,0:T(8,128)} fusion(f32[16384,5]{1,0:T(8,128)} %get-tuple-element.617, f32[16384,5]{1,0:T(8,128)} %get-tuple-element.616, f32[16384,5]{1,0:T(8,128)} %get-tuple-element.615, f32[16384,5]{1,0:T(8,128)} %bitcast.214), kind=kLoop, calls=%fused_computation.95 | loop fusion | flops 983040 | bytes 2621440 | tf_op jit(solution)/shard_map/concatenate | solution.py:65
  847.6 57.8 %gather_fusion.6 = f32[16384,20]{1,0:T(8,128)} fusion(f32[16384,20]{1,0:T(8,128)} %pad_maximum_fusion.3, s32[16384]{0:T(1024)S(1)} %copy-done.14), kind=kCustom, calls=%fused_computation.4.clone | custom fusion | bytes 2686976 | tf_op jit(solution)/shard_map/jit(_take)/gather | solution.py:74
  905.4 6.3 copy.154
  915.5 22.9 %all_to_all.22 = f32[5,64,256]{2,0,1:T(8,128)S(1)} all-to-all(f32[5,64,256]{2,0,1:T(8,128)S(1)} %copy.155), channel_id=1, replica_groups=mesh['group'=2,'blk'=64] {'blk'}, dimensions={1} | all-to-all | bytes 655360 | tf_op jit(solution)/shard_map/all_to_all | solution.py:120
  943.2 7.8 pad.64
  951.0 57.8 %gather_fusion.7 = f32[16384,5]{1,0:T(8,128)} fusion(f32[16385,5]{1,0:T(8,128)} %pad.64, s32[16384]{0:T(1024)S(1)} %copy-done.18), kind=kCustom, calls=%fused_computation.7.clone | custom fusion | bytes 720896 | tf_op jit(solution)/shard_map/jit(_take)/gather | solution.py:122
  1008.8 9.5 bitcast_select_fusion
  1026.0 7.7 collective-permute-start.17
  1035.6 6.7 conditional.14
  1045.3 8.5 collective-permute-start.19
  (212 shorter events, 139.8 us)
Async XLA Ops:
  0.9 104.8 %copy-start.19 = (pred[16384]{0:T(1024)(128)(4,1)}, pred[16384]{0:T(1024)(128)(4,1)S(1)}, u32[]{:S(2)}) copy-start(pred[16384]{0:T(1024)(128)(4,1)S(1)} %compare_and_fusion.1) | copy-start | bytes 49156
  0.9 41.3 %copy-start.11 = (s32[16384]{0:T(1024)}, s32[16384]{0:T(1024)S(1)}, u32[]{:S(2)}) copy-start(s32[16384]{0:T(1024)S(1)} %fusion.18) | copy-start | bytes 196612
  2.1 103.8 %copy-start.3 = (f32[8,2,8,128]{3,1,2,0:T(2,128)}, f32[8,2,8,128]{3,1,2,0:T(2,128)S(1)}, u32[]{:S(2)}) copy-start(f32[8,2,8,128]{3,1,2,0:T(2,128)S(1)} %copy.167) | copy-start | bytes 196612
  2.1 103.7 %copy-start.7 = (f32[8,2,8,128]{3,1,2,0:T(2,128)}, f32[8,2,8,128]{3,1,2,0:T(2,128)S(1)}, u32[]{:S(2)}) copy-start(f32[8,2,8,128]{3,1,2,0:T(2,128)S(1)} %copy.166) | copy-start | bytes 196612
  106.2 60.7 %collective-permute-start = (f32[5,64,256]{2,1,0:T(8,128)S(1)}, f32[5,64,256]{2,1,0:T(8,128)S(1)}, u32[]{:S(2)}, u32[]{:S(2)}) collective-permute-start(f32[5,64,256]{2,1,0:T(8,128)S(1)} %bitcast.277), channel_id=1, source_target_pairs={{0,64},{64,0},{1,65},{65,1},{2,66},{66,2},{3,67},{67,3},{4,68},{68... | collective-permute-start | bytes 983048 | tf_op jit(solution)/shard_map/ppermute | solution.py:16
  166.9 95.8 %copy-start.23 = (pred[16384]{0:T(1024)(128)(4,1)}, pred[16384]{0:T(1024)(128)(4,1)S(1)}, u32[]{:S(2)}) copy-start(pred[16384]{0:T(1024)(128)(4,1)S(1)} %get-tuple-element.566) | copy-start | bytes 49156
  166.9 95.8 %copy-start.27 = (pred[16384]{0:T(1024)(128)(4,1)}, pred[16384]{0:T(1024)(128)(4,1)S(1)}, u32[]{:S(2)}) copy-start(pred[16384]{0:T(1024)(128)(4,1)S(1)} %get-tuple-element.647) | copy-start | bytes 49156
  168.0 24.0 %all-to-all-start = ((f32[5,64,256]{2,0,1:T(8,128)}), f32[5,64,256]{2,0,1:T(8,128)S(1)}, u32[]{:S(2)}, u32[]{:S(2)}) async-start(f32[5,64,256]{2,0,1:T(8,128)} %copy.128), calls=%async_computation | async-start | bytes 1048576 | tf_op jit(solution)/shard_map/all_to_all | solution.py:120
  179.1 25.5 %copy-start.15 = (s32[16384]{0:T(1024)}, s32[16384]{0:T(1024)S(1)}, u32[]{:S(2)}) copy-start(s32[16384]{0:T(1024)S(1)} %fusion.19) | copy-start | bytes 196612
  272.2 17.5 %copy-start = (f32[1,1,5,5,32,512]{5,4,3,2,1,0:T(8,128)S(1)}, f32[1,1,5,5,32,512]{5,4,3,2,1,0:T(8,128)}, u32[]{:S(2)}) copy-start(f32[1,1,5,5,32,512]{5,4,3,2,1,0:T(8,128)} %param.29) | copy-start | bytes 4915204
  272.2 17.5 %copy-start.1 = (f32[1,1,5,32,512]{4,3,2,1,0:T(8,128)S(1)}, f32[1,1,5,32,512]{4,3,2,1,0:T(8,128)}, u32[]{:S(2)}) copy-start(f32[1,1,5,32,512]{4,3,2,1,0:T(8,128)} %param.28) | copy-start | bytes 983044
  272.2 17.5 %copy-start.2 = (f32[1,1,4,32,512]{4,3,2,1,0:T(8,128)S(1)}, f32[1,1,4,32,512]{4,3,2,1,0:T(8,128)}, u32[]{:S(2)}) copy-start(f32[1,1,4,32,512]{4,3,2,1,0:T(8,128)} %param.30) | copy-start | bytes 786436
  277.7 10.7 %collective-permute-start.1 = (f32[5,3,512]{2,1,0:T(4,128)S(1)}, f32[5,3,512]{2,1,0:T(4,128)S(1)}, u32[]{:S(2)}, u32[]{:S(2)}) collective-permute-start(f32[5,3,512]{2,1,0:T(4,128)S(1)} %get-tuple-element.641), channel_id=1, source_target_pairs={{0,1},{1,2},{2,3},{3,4},{4,5},{5,6},{6,7},{7,8},{8,9},{9,10},{10,1... | collective-permute-start | bytes 92168 | tf_op jit(solution)/shard_map/ppermute | solution.py:24
  280.1 9.3 collective-permute-start.2
  297.7 10.4 collective-permute-start.3
  299.7 10.1 collective-permute-start.4
  333.3 17.0 %copy-start.12 = (s32[16384]{0:T(1024)S(1)}, s32[16384]{0:T(1024)}, u32[]{:S(2)}) copy-start(s32[16384]{0:T(1024)} %copy-done.11) | copy-start | bytes 196612
  408.2 7.8 copy-start.4
  408.2 7.8 copy-start.8
  416.4 1.7 collective-permute-start.5
  453.9 57.8 %copy-start.24 = (pred[16384]{0:T(1024)(128)(4,1)S(1)}, pred[16384]{0:T(1024)(128)(4,1)}, u32[]{:S(2)}) copy-start(pred[16384]{0:T(1024)(128)(4,1)} %copy-done.23) | copy-start | bytes 49156
  454.0 57.8 %copy-start.28 = (pred[16384]{0:T(1024)(128)(4,1)S(1)}, pred[16384]{0:T(1024)(128)(4,1)}, u32[]{:S(2)}) copy-start(pred[16384]{0:T(1024)(128)(4,1)} %copy-done.27) | copy-start | bytes 49156
  526.5 10.1 collective-permute-start.6
  528.9 9.3 collective-permute-start.7
  546.4 10.4 collective-permute-start.8
  548.3 10.1 collective-permute-start.9
  582.1 17.0 %copy-start.13 = (s32[16384]{0:T(1024)S(1)}, s32[16384]{0:T(1024)}, u32[]{:S(2)}) copy-start(s32[16384]{0:T(1024)} %copy-done.11) | copy-start | bytes 196612
  656.9 7.8 copy-start.5
  656.9 7.8 copy-start.9
  665.2 1.7 collective-permute-start.10
  702.3 57.8 %copy-start.25 = (pred[16384]{0:T(1024)(128)(4,1)S(1)}, pred[16384]{0:T(1024)(128)(4,1)}, u32[]{:S(2)}) copy-start(pred[16384]{0:T(1024)(128)(4,1)} %copy-done.23) | copy-start | bytes 49156
  702.3 57.8 %copy-start.29 = (pred[16384]{0:T(1024)(128)(4,1)S(1)}, pred[16384]{0:T(1024)(128)(4,1)}, u32[]{:S(2)}) copy-start(pred[16384]{0:T(1024)(128)(4,1)} %copy-done.27) | copy-start | bytes 49156
  774.9 10.1 collective-permute-start.11
  777.3 9.3 collective-permute-start.12
  795.0 10.4 collective-permute-start.13
  796.9 10.1 collective-permute-start.14
  830.6 17.0 %copy-start.14 = (s32[16384]{0:T(1024)S(1)}, s32[16384]{0:T(1024)}, u32[]{:S(2)}) copy-start(s32[16384]{0:T(1024)} %copy-done.11) | copy-start | bytes 196612
  905.4 7.8 copy-start.6
  905.4 7.8 copy-start.10
  913.6 1.7 collective-permute-start.15
  951.0 57.8 %copy-start.26 = (pred[16384]{0:T(1024)(128)(4,1)S(1)}, pred[16384]{0:T(1024)(128)(4,1)}, u32[]{:S(2)}) copy-start(pred[16384]{0:T(1024)(128)(4,1)} %copy-done.23) | copy-start | bytes 49156
  951.0 57.8 %copy-start.30 = (pred[16384]{0:T(1024)(128)(4,1)S(1)}, pred[16384]{0:T(1024)(128)(4,1)}, u32[]{:S(2)}) copy-start(pred[16384]{0:T(1024)(128)(4,1)} %copy-done.27) | copy-start | bytes 49156
  1018.3 17.3 %copy-start.32 = (pred[32,512]{1,0:T(8,128)(4,1)S(1)}, pred[32,512]{1,0:T(8,128)(4,1)}, u32[]{:S(2)}) copy-start(pred[32,512]{1,0:T(8,128)(4,1)} %get-tuple-element.649) | copy-start | bytes 49156
  1023.6 10.1 collective-permute-start.16
  1026.0 9.3 collective-permute-start.17
  1035.6 20.1 %copy-start.31 = (pred[32,512]{1,0:T(8,128)(4,1)S(1)}, pred[32,512]{1,0:T(8,128)(4,1)}, u32[]{:S(2)}) copy-start(pred[32,512]{1,0:T(8,128)(4,1)} %get-tuple-element.648) | copy-start | bytes 49156
  1043.4 10.4 collective-permute-start.18
  1045.3 10.1 collective-permute-start.19
  (11 other events, 64.7 us)
where the time goes:
time: 1070 us; the launch traced here: 1060 us
  local copies, waits for them, and re-layouts  736 us (69%)
  other arithmetic  127 us (12%)
  starting transfers between devices  93.2 us (9%)
  blocking collectives  68.5 us (6%)
  waiting for transfers between devices  30.3 us (3%)
    gather x8, local copies, waits for them, and re-layouts, interpolate(): picked = jnp.take(corner_table, row_bases, axis=0)  256 us
    gather x4, local copies, waits for them, and re-layouts, on_device(): placed = jnp.take(arrived_rows, slot_of_cell, axis=0).T  232 us
    all_to_all x3, blocking collectives, on_device(): lax.all_to_all(crossed, 'blk', split_axis=1, concat_axis=1, tiled=True)  68.5 us
    slice x4, local copies, waits for them, and re-layouts, interpolate(): cell_major[1:cell_count + 1]  68.1 us
    concatenate x4, other arithmetic, interpolate(): jnp.concatenate([cell_major[0:cell_count], cell_major[1:cell_count + 1],...  68.1 us
    ppermute x8, starting transfers between devices, padded_2(): lax.ppermute(lax.slice_in_dim(block, 0, width, axis=dim), axis, backward)  64.5 us
    scatter x1, local copies, waits for them, and re-layouts, on_device(): slot_of_cell = jnp.full((cell_count,), slot_total, jnp.int32).at[targets]...  60.3 us
    select_n x4, other arithmetic, on_device(): flat_state = jnp.where(frozen_flat[None], placed, flat_state)  37.9 us
  transfers between devices with their start and end apart: 21, of which 12 were waited for; matrix products, arithmetic and copies ran while one was open for 6% of the time, Pallas kernels for 0%

commit v1 on v0

v1 whole, which is shorter than its diff:
```python
import functools

import jax
import jax.numpy as jnp
from jax import lax
from jax.experimental import pallas as pl
from jax.experimental.pallas import tpu as pltpu
from jax.sharding import PartitionSpec as P

ITERS = 4
V = 5
NJ = 32
NK = 512
S = 256
TOP = 8
G = 8

upwind_offsets = (-3, -2, -1, 0, 1, 2)
upwind_weights = (-2.0 / 60.0, 15.0 / 60.0, -60.0 / 60.0, 20.0 / 60.0, 30.0 / 60.0, -3.0 / 60.0)

f32, bf16, i32 = jnp.float32, jnp.bfloat16, jnp.int32
MESH = pl.DeviceIdType.MESH


def shift_k(x, o):
    if o == 0:
        return x
    n = x.shape[1]
    col = lax.broadcasted_iota(i32, x.shape, 1)
    rolled = pltpu.roll(x, (-o) % n, axis=1)
    keep = (col + o >= 0) & (col + o < n)
    return jnp.where(keep, rolled, 0.0)


def split(x):
    hi = x.astype(bf16)
    return hi, (x - hi.astype(f32)).astype(bf16)


def make_table(u, tab):
    zero = jnp.zeros((1, 1), f32)
    for v in range(V):
        a = u[0, v, TOP : TOP + NJ, :]
        first = jnp.concatenate([a[1:, :1], zero], axis=0)
        b = jnp.concatenate([a[:, 1:], first], axis=1)
        for i, t in enumerate((a, b)):
            hi, lo = split(t)
            tab[pl.ds(320 * i + 32 * v, 32), :] = hi
            tab[pl.ds(320 * i + 160 + 32 * v, 32), :] = lo


def interpolate(tab, base, w):
    k = base & (NK - 1)
    j = base >> 9
    hot = jnp.where(lax.broadcasted_iota(i32, (NK, S), 0) == k, 1.0, 0.0).astype(bf16)
    g = jnp.dot(tab[...], hot, preferred_element_type=f32)
    row = lax.broadcasted_iota(i32, (NJ, S), 0)
    here, below = row == j, row == j + 1
    p0 = jnp.where(here, w[0], jnp.where(below, w[2], 0.0))
    p1 = jnp.where(here, w[1], jnp.where(below, w[3], 0.0))
    rows = []
    for v in range(V):
        a = g[32 * v : 32 * v + 32] + g[160 + 32 * v : 192 + 32 * v]
        b = g[320 + 32 * v : 352 + 32 * v] + g[480 + 32 * v : 512 + 32 * v]
        rows.append(jnp.sum(a * p0 + b * p1, axis=0, keepdims=True))
    return jnp.concatenate(rows + [jnp.zeros((3, S), f32)], axis=0)


def kernel(
    blocks,
    field, source, inverse, coupling, base, weight, cell,
    out,
    u, tab, send, recv, acc, frozen, part, hsend, hrecv,
    send_sem, recv_sem, hsend_sem, hrecv_sem,
):
    g = lax.axis_index("group")
    b = lax.axis_index("blk")
    groups = blocks // G
    mine, within = b // G, b % G
    other = 1 - g
    is_near = g == 0
    has_low, has_high = b > 0, b < blocks - 1

    barrier = pltpu.get_barrier_semaphore()

    def greet(d, c):
        pl.semaphore_signal(barrier, inc=1, device_id=(other, d), device_id_type=MESH)
        return c

    lax.fori_loop(0, blocks, greet, 0)

    for d in ((b + blocks - 1) % blocks, (b + 1) % blocks):
        pl.semaphore_signal(barrier, inc=1, device_id=(g, d), device_id_type=MESH)

    for s in range(2):
        for v in range(V):
            u[s, v, 0:TOP, :] = jnp.zeros((TOP, NK), f32)
            u[s, v, TOP + NJ : TOP + NJ + 8, :] = jnp.zeros((8, NK), f32)
    for v in range(V):
        u[0, v, TOP : TOP + NJ, :] = field[v]
    hsend[...] = jnp.zeros_like(hsend)

    pl.semaphore_wait(barrier, blocks + 2)

    def message(it, i, d):
        return pltpu.make_async_remote_copy(
            src_ref=send.at[d],
            dst_ref=recv.at[it, b],
            send_sem=send_sem,
            recv_sem=recv_sem.at[it, i],
            device_id=(other, d),
            device_id_type=MESH,
        )

    def halo(n, side, target):
        return pltpu.make_async_remote_copy(
            src_ref=hsend.at[side],
            dst_ref=hrecv.at[n, 1 - side],
            send_sem=hsend_sem.at[side],
            recv_sem=hrecv_sem.at[n, 1 - side],
            device_id=(g, target),
            device_id_type=MESH,
        )

    for it in range(ITERS):
        make_table(u, tab)

        def gather_group(i, c):
            dg = (mine + i) % groups
            first = pl.multiple_of(dg * G, G)
            bases = base[pl.ds(first, G), :]
            ws = [weight[q, pl.ds(first, G), :] for q in range(4)]
            for q in range(G):
                send[first + q] = interpolate(
                    tab, bases[q : q + 1], [w[q : q + 1] for w in ws]
                )
            for q in range(G):
                message(it, i, first + (within + q) % G).start()
            return c

        lax.fori_loop(0, groups, gather_group, 0)

        acc[...] = jnp.zeros_like(acc)
        if it == 0:
            frozen[...] = jnp.zeros_like(frozen)

        def scatter_group(i, c):
            sg = (mine + groups - i) % groups
            first = pl.multiple_of(sg * G, G)
            pltpu.make_async_copy(
                recv.at[it, pl.ds(first, G)], recv.at[it, pl.ds(first, G)], recv_sem.at[it, i]
            ).wait()
            cells = cell[pl.ds(first, G), :]
            left, right = [], []
            for q in range(G):
                r = cells[q : q + 1]
                hit = lax.broadcasted_iota(i32, (NJ, S), 0) == (r >> 9)
                val = recv[it, first + q]
                hi = val.astype(bf16).astype(f32)
                rows = [
                    jnp.where(hit, t[v : v + 1], 0.0) for t in (hi, val - hi) for v in range(V)
                ]
                if it == 0:
                    rows.append(jnp.where(hit, 1.0, 0.0))
                left.append(jnp.concatenate(rows, axis=0).astype(bf16))
                right.append(
                    jnp.where(
                        lax.broadcasted_iota(i32, (NK, S), 0) == (r & (NK - 1)), 1.0, 0.0
                    ).astype(bf16)
                )
            p = lax.dot_general(
                jnp.concatenate(left, axis=1),
                jnp.concatenate(right, axis=1),
                (((1,), (1,)), ((), ())),
                preferred_element_type=f32,
            )
            acc[...] += p[:320]
            if it == 0:
                frozen[...] += p[320:]
            return c

        lax.fori_loop(0, groups, scatter_group, 0)

        pltpu.make_async_copy(send, send, send_sem).wait()

        fixed = frozen[...] > 0.5
        for v in range(V):
            placed = acc[32 * v : 32 * v + 32] + acc[160 + 32 * v : 192 + 32 * v]
            u[0, v, TOP : TOP + NJ, :] = jnp.where(fixed, placed, u[0, v, TOP : TOP + NJ, :])

        def half(h, c):
            n = 2 * it + h
            for v in range(V):
                hsend[0, 3 * v : 3 * v + 3, :] = u[h, v, TOP : TOP + 3, :]
                hsend[1, 3 * v : 3 * v + 3, :] = u[h, v, TOP + NJ - 3 : TOP + NJ, :]

            @pl.when(has_low)
            def _():
                halo(n, 0, b - 1).start()

            @pl.when(has_high)
            def _():
                halo(n, 1, b + 1).start()

            @pl.when(is_near)
            def _():
                for t in range(4):
                    rows = slice(8 * t, 8 * t + 8)
                    for v in range(V):
                        x = u[h, v, TOP + 8 * t : TOP + 8 * t + 8, :]
                        part[v, rows, :] = (
                            source[v, rows, :]
                            + coupling[2, rows, :] * shift_k(x, -1)
                            + coupling[3, rows, :] * shift_k(x, 1)
                        )

            @pl.when(jnp.logical_not(is_near))
            def _():
                for t in range(4):
                    rows = slice(8 * t, 8 * t + 8)
                    for v in range(V):
                        x = u[h, v, TOP + 8 * t : TOP + 8 * t + 8, :]
                        along = sum(a * shift_k(x, o) for o, a in zip(upwind_offsets, upwind_weights))
                        part[v, rows, :] = source[v, rows, :] - coupling[1, rows, :] * along

            @pl.when(has_low)
            def _():
                halo(n, 1, b - 1).wait_recv()
                for v in range(V):
                    u[h, v, TOP - 3 : TOP, :] = hrecv[n, 0, 3 * v : 3 * v + 3, :]

            @pl.when(has_high)
            def _():
                halo(n, 0, b + 1).wait_recv()
                for v in range(V):
                    u[h, v, TOP + NJ : TOP + NJ + 3, :] = hrecv[n, 1, 3 * v : 3 * v + 3, :]

            def apply(rows, ts, v):
                return sum(inverse[v, w, rows, :] * ts[w] for w in range(V))

            @pl.when(is_near)
            def _():
                for t in range(4):
                    rows = slice(8 * t, 8 * t + 8)
                    at = TOP + 8 * t
                    ts = [
                        part[v, rows, :]
                        + coupling[0, rows, :] * u[h, v, at - 1 : at + 7, :]
                        + coupling[1, rows, :] * u[h, v, at + 1 : at + 9, :]
                        for v in range(V)
                    ]
                    parity = (
                        lax.broadcasted_iota(i32, (8, NK), 0) + lax.broadcasted_iota(i32, (8, NK), 1) + h
                    ) % 2
                    update = (frozen[rows, :] < 0.5) & (parity == 0)
                    for v in range(V):
                        u[1 - h, v, at : at + 8, :] = jnp.where(
                            update, apply(rows, ts, v), u[h, v, at : at + 8, :]
                        )

            @pl.when(jnp.logical_not(is_near))
            def _():
                for t in range(4):
                    rows = slice(8 * t, 8 * t + 8)
                    at = TOP + 8 * t
                    ts = []
                    for v in range(V):
                        along = sum(
                            a * u[h, v, at + o : at + o + 8, :]
                            for o, a in zip(upwind_offsets, upwind_weights)
                        )
                        ts.append(part[v, rows, :] - coupling[0, rows, :] * along)
                    update = frozen[rows, :] < 0.5
                    for v in range(V):
                        old = u[h, v, at : at + 8, :]
                        u[1 - h, v, at : at + 8, :] = jnp.where(update, old + apply(rows, ts, v), old)

            @pl.when(has_low)
            def _():
                halo(n, 0, b - 1).wait_send()

            @pl.when(has_high)
            def _():
                halo(n, 1, b + 1).wait_send()

            return c

        lax.fori_loop(0, 2, half, 0)

    for v in range(V):
        out[v] = u[0, v, TOP : TOP + NJ, :]


def on_device(field, source, block_inverse, coupling, donor_base, donor_weight, receiver_cell):
    blocks = donor_base.shape[2]
    vmem = pl.BlockSpec(memory_space=pltpu.VMEM)
    result = pl.pallas_call(
        functools.partial(kernel, blocks),
        out_shape=jax.ShapeDtypeStruct((V, NJ, NK), f32),
        in_specs=[vmem] * 7,
        out_specs=vmem,
        scratch_shapes=[
            pltpu.VMEM((2, V, TOP + NJ + 8, NK), f32),
            pltpu.VMEM((640, NK), bf16),
            pltpu.VMEM((blocks, 8, S), f32),
            pltpu.VMEM((ITERS, blocks, 8, S), f32),
            pltpu.VMEM((320, NK), f32),
            pltpu.VMEM((NJ, NK), f32),
            pltpu.VMEM((V, NJ, NK), f32),
            pltpu.VMEM((2, 16, NK), f32),
            pltpu.VMEM((2 * ITERS, 2, 16, NK), f32),
            pltpu.SemaphoreType.DMA,
            pltpu.SemaphoreType.DMA((ITERS, blocks // G)),
            pltpu.SemaphoreType.DMA((2,)),
            pltpu.SemaphoreType.DMA((2 * ITERS, 2)),
        ],
        compiler_params=pltpu.CompilerParams(
            collective_id=0, has_side_effects=True, vmem_limit_bytes=48 * 2**20
        ),
    )(
        field[0, 0],
        source[0, 0],
        block_inverse[0, 0],
        coupling[0, 0],
        donor_base[0, 0],
        donor_weight[0, 0],
        receiver_cell[0, 0],
    )
    return result[None, None]


def solution(mesh):
    in_specs = (
        P("group", "blk", None, None, None),
        P("group", "blk", None, None, None),
        P("group", "blk", None, None, None, None),
        P("group", "blk", None, None, None),
        P("group", "blk", None, None),
        P("group", "blk", None, None, None),
        P("group", "blk", None, None),
    )
    out_specs = P("group", "blk", None, None, None)
    return jax.shard_map(
        on_device, mesh=mesh, in_specs=in_specs, out_specs=out_specs, check_vma=False
    )
```

time: 1070 us -> 142 us (0.13); the launches traced: 1060 us -> 142 us
  local copies, waits for them, and re-layouts: 736 us -> 7.68 us
  Pallas kernels: 0 us -> 134 us
  other arithmetic: 127 us -> 0 us
  starting transfers between devices: 93.2 us -> 0 us
  blocking collectives: 68.5 us -> 0 us
  waiting for transfers between devices: 30.3 us -> 0 us
    gather x12 -> x0, local copies, waits for them, and re-layouts: 487 us -> none  [the longest x8 256 us: interpolate(): picked = jnp.take(corner_table, row_bases, axis=0)]
    pallas_call x0 -> x1, Pallas kernels: none -> 134 us  [on_device(): pl.pallas_call(functools.partial(kernel, blocks), out_shape=jax.ShapeDtyp...]
    ppermute x20 -> x0, starting transfers between devices: 82.1 us -> none  [the longest x8 64.5 us: padded_2(): lax.ppermute(lax.slice_in_dim(block, 0, width, axis=dim), axis, backward)]
    concatenate x12 -> x0, other arithmetic: 70.2 us -> none  [the longest x4 68.1 us: interpolate(): jnp.concatenate([cell_major[0:cell_count], cell_major[1:cell_count + 1],...]
    all_to_all x3 -> x0, blocking collectives: 68.5 us -> none  [on_device(): lax.all_to_all(crossed, 'blk', split_axis=1, concat_axis=1, tiled=True)]
    slice x12 -> x0, local copies, waits for them, and re-layouts: 68.2 us -> none  [the longest x4 68.1 us: interpolate(): cell_major[1:cell_count + 1]]
    scatter x1 -> x0, local copies, waits for them, and re-layouts: 60.3 us -> none  [on_device(): slot_of_cell = jnp.full((cell_count,), slot_total, jnp.int32).at[targets]...]
    select_n x16 -> x0, other arithmetic: 47.1 us -> none  [the longest x4 37.9 us: on_device(): flat_state = jnp.where(frozen_flat[None], placed, flat_state)]
  transfers between devices with their start and end apart: 21 -> 0, of which waited for: 12 -> 0; matrix products, arithmetic and copies ran while one was open for 6% -> 0% of each run, Pallas kernels for 0% -> 0%
where the time goes in v1:
time: 142 us
  Pallas kernels  134 us (94%)
  local copies, waits for them, and re-layouts  7.68 us (5%)
    pallas_call x1, Pallas kernels, on_device(): pl.pallas_call(functools.partial(kernel, blocks), out_shape=jax.ShapeDtyp...  134 us
    unnamed x15, local copies, waits for them, and re-layouts  7.68 us

profile of v1, /device:TPU:32, one launch (start us, length us, event | category | flops | bytes accessed | tf_op | source)
XLA Modules:
  0.0 142.1 jit_solution(428325550281171778)
XLA Ops:
  0.0 0.0 copy-start
  0.0 1.4 %copy-done = f32[1,1,5,5,32,512]{5,4,3,2,1,0:T(8,128)S(1)} copy-done((f32[1,1,5,5,32,512]{5,4,3,2,1,0:T(8,128)S(1)}, f32[1,1,5,5,32,512]{5,4,3,2,1,0:T(8,128)}, u32[]{:S(2)}) %copy-start) | copy-done | bytes 1638424
  1.4 0.0 copy-start.1
  1.4 1.0 copy-done.1
  2.4 0.0 copy-start.2
  2.4 1.0 copy-done.2
  3.4 0.0 copy-start.3
  3.4 0.9 copy-done.3
  4.3 0.0 copy-start.4
  4.3 0.9 copy-done.4
  5.3 0.0 copy-start.5
  5.3 0.8 copy-done.5
  6.1 0.0 copy-start.6
  6.1 0.8 copy-done.6
  7.0 134.4 %shard_map.73 = f32[5,32,512]{2,1,0:T(8,128)S(1)} custom-call(f32[5,32,512]{2,1,0:T(8,128)S(1)} %bitcast.10, f32[5,32,512]{2,1,0:T(8,128)S(1)} %bitcast.11, f32[5,5,32,512]{3,2,1,0:T(8,128)S(1)} %bitcast.8, f32[4,32,512]{2,1,0:T(8,128)S(1)} %bitcast.12, s32[64,256]{1,0:T(8,128)S(1)} %bitcast.14, f32[4,64,256]{2,1,0:T(8,128)S(1)} %bitcast.13, ...), custom_call_target="tpu_custom_call" | custom-call | tf_op jit(solution)/shard_map/pallas_call | solution.py:297
  141.3 0.7 copy.9
Async XLA Ops:
  0.0 1.4 %copy-start = (f32[1,1,5,5,32,512]{5,4,3,2,1,0:T(8,128)S(1)}, f32[1,1,5,5,32,512]{5,4,3,2,1,0:T(8,128)}, u32[]{:S(2)}) copy-start(f32[1,1,5,5,32,512]{5,4,3,2,1,0:T(8,128)} %param.9) | copy-start | bytes 4915204
  1.4 1.0 copy-start.1
  2.4 1.0 copy-start.2
  3.4 0.9 copy-start.3
  4.3 0.9 copy-start.4
  5.3 0.8 copy-start.5
  6.1 0.8 copy-start.6

commit v2 on v1

--- a/solution.py
+++ b/solution.py
@@ -38,40 +38,67 @@
 
 
 def make_table(u, tab):
-    zero = jnp.zeros((1, 1), f32)
     for v in range(V):
-        a = u[0, v, TOP : TOP + NJ, :]
-        first = jnp.concatenate([a[1:, :1], zero], axis=0)
-        b = jnp.concatenate([a[:, 1:], first], axis=1)
-        for i, t in enumerate((a, b)):
-            hi, lo = split(t)
-            tab[pl.ds(320 * i + 32 * v, 32), :] = hi
-            tab[pl.ds(320 * i + 160 + 32 * v, 32), :] = lo
-
-
-def interpolate(tab, base, w):
-    k = base & (NK - 1)
-    j = base >> 9
-    hot = jnp.where(lax.broadcasted_iota(i32, (NK, S), 0) == k, 1.0, 0.0).astype(bf16)
+        hl = jnp.concatenate(split(u[0, v, TOP : TOP + NJ, :]), axis=0)
+        for e in range(2):
+            pick = jnp.where(
+                lax.broadcasted_iota(i32, (NK, NK // 2), 0)
+                == 2 * lax.broadcasted_iota(i32, (NK, NK // 2), 1) + e,
+                1.0,
+                0.0,
+            ).astype(bf16)
+            t = jnp.dot(hl, pick, preferred_element_type=f32)
+            parts = [(e, t)]
+            if e == 0:
+                first = jnp.concatenate([t[1:, :1], jnp.zeros((1, 1), f32)], axis=0)
+                parts.append((2, jnp.concatenate([t[:, 1:], first], axis=1)))
+            for o, p in parts:
+                p = p.astype(bf16)
+                tab[pl.ds(160 * o + 32 * v, 32), :] = p[:32]
+                tab[pl.ds(480 + 160 * o + 32 * v, 32), :] = p[32:]
+
+
+def one_hot(base):
+    k = (base & (NK - 1)) >> 1
+    return jnp.where(lax.broadcasted_iota(i32, (NK // 2, S), 0) == k, 1.0, 0.0).astype(bf16)
+
+
+def patterns(base, w):
+    even = (base & 1) == 0
+    row = lax.broadcasted_iota(i32, (NJ, S), 0)
+    here, below = row == (base >> 9), row == (base >> 9) + 1
+    zero = jnp.zeros_like(w[0])
+
+    def spread(x, y):
+        return jnp.where(here, x, jnp.where(below, y, 0.0))
+
+    return (
+        spread(jnp.where(even, w[0], zero), jnp.where(even, w[2], zero)),
+        spread(jnp.where(even, w[1], w[0]), jnp.where(even, w[3], w[2])),
+        spread(jnp.where(even, zero, w[1]), jnp.where(even, zero, w[3])),
+    )
+
+
+def interpolate(tab, hot, ps):
     g = jnp.dot(tab[...], hot, preferred_element_type=f32)
-    row = lax.broadcasted_iota(i32, (NJ, S), 0)
-    here, below = row == j, row == j + 1
-    p0 = jnp.where(here, w[0], jnp.where(below, w[2], 0.0))
-    p1 = jnp.where(here, w[1], jnp.where(below, w[3], 0.0))
     rows = []
     for v in range(V):
-        a = g[32 * v : 32 * v + 32] + g[160 + 32 * v : 192 + 32 * v]
-        b = g[320 + 32 * v : 352 + 32 * v] + g[480 + 32 * v : 512 + 32 * v]
-        rows.append(jnp.sum(a * p0 + b * p1, axis=0, keepdims=True))
+        total = None
+        for o in range(3):
+            at = 160 * o + 32 * v
+            term = (g[at : at + 32] + g[480 + at : 512 + at]) * ps[o]
+            total = term if total is None else total + term
+        rows.append(jnp.sum(total, axis=0, keepdims=True))
     return jnp.concatenate(rows + [jnp.zeros((3, S), f32)], axis=0)
 
 
 def kernel(
     blocks,
-    field, source, inverse, coupling, base, weight, cell,
+    field_hbm, source_hbm, inverse_hbm, coupling_hbm, base_hbm, weight_hbm, cell_hbm,
     out,
-    u, tab, send, recv, acc, frozen, part, hsend, hrecv,
-    send_sem, recv_sem, hsend_sem, hrecv_sem,
+    source, inverse, coupling, base, weight, cell,
+    u, tab, hots, pats, send, recv, acc, frozen, part, hsend, hrecv,
+    send_sem, recv_sem, hsend_sem, hrecv_sem, in_sem,
 ):
     g = lax.axis_index("group")
     b = lax.axis_index("blk")
@@ -81,6 +108,26 @@
     is_near = g == 0
     has_low, has_high = b > 0, b < blocks - 1
 
+    def block_rows(ref):
+        return ref.at[0, :, pl.ds(TOP, NJ), :]
+
+    loads = [
+        pltpu.make_async_copy(a, c, in_sem.at[n])
+        for n, (a, c) in enumerate(
+            (
+                (field_hbm, block_rows(u)),
+                (base_hbm, base),
+                (weight_hbm, weight),
+                (cell_hbm, cell),
+                (source_hbm, source),
+                (coupling_hbm, coupling),
+                (inverse_hbm, inverse),
+            )
+        )
+    ]
+    for load in loads:
+        load.start()
+
     barrier = pltpu.get_barrier_semaphore()
 
     def greet(d, c):
@@ -96,11 +143,10 @@
         for v in range(V):
             u[s, v, 0:TOP, :] = jnp.zeros((TOP, NK), f32)
             u[s, v, TOP + NJ : TOP + NJ + 8, :] = jnp.zeros((8, NK), f32)
-    for v in range(V):
-        u[0, v, TOP : TOP + NJ, :] = field[v]
     hsend[...] = jnp.zeros_like(hsend)
 
-    pl.semaphore_wait(barrier, blocks + 2)
+    for load in loads[:3]:
+        load.wait()
 
     def message(it, i, d):
         return pltpu.make_async_remote_copy(
@@ -128,12 +174,26 @@
         def gather_group(i, c):
             dg = (mine + i) % groups
             first = pl.multiple_of(dg * G, G)
-            bases = base[pl.ds(first, G), :]
-            ws = [weight[q, pl.ds(first, G), :] for q in range(4)]
+            if it == 0:
+                bases = base[pl.ds(first, G), :]
+                ws = [weight[q, pl.ds(first, G), :] for q in range(4)]
             for q in range(G):
-                send[first + q] = interpolate(
-                    tab, bases[q : q + 1], [w[q : q + 1] for w in ws]
-                )
+                if it == 0:
+                    hot = one_hot(bases[q : q + 1])
+                    ps = patterns(bases[q : q + 1], [w[q : q + 1] for w in ws])
+                    hots[first + q] = hot
+                    for o in range(3):
+                        pats[first + q, o] = ps[o]
+                else:
+                    hot = hots[first + q]
+                    ps = [pats[first + q, o] for o in range(3)]
+                send[first + q] = interpolate(tab, hot, ps)
+            if it == 0:
+
+                @pl.when(i == 0)
+                def _():
+                    pl.semaphore_wait(barrier, blocks + 2)
+
             for q in range(G):
                 message(it, i, first + (within + q) % G).start()
             return c
@@ -143,6 +203,7 @@
         acc[...] = jnp.zeros_like(acc)
         if it == 0:
             frozen[...] = jnp.zeros_like(frozen)
+            loads[3].wait()
 
         def scatter_group(i, c):
             sg = (mine + groups - i) % groups
@@ -188,6 +249,10 @@
             placed = acc[32 * v : 32 * v + 32] + acc[160 + 32 * v : 192 + 32 * v]
             u[0, v, TOP : TOP + NJ, :] = jnp.where(fixed, placed, u[0, v, TOP : TOP + NJ, :])
 
+        if it == 0:
+            for load in loads[4:]:
+                load.wait()
+
         def half(h, c):
             n = 2 * it + h
             for v in range(V):
@@ -202,26 +267,73 @@
             def _():
                 halo(n, 1, b + 1).start()
 
+            def apply(rows, ts, v):
+                return sum(inverse[v, w, rows, :] * ts[w] for w in range(V))
+
+            def near_k(v, rows, at):
+                x = u[h, v, at : at + 8, :]
+                return (
+                    source[v, rows, :]
+                    + coupling[2, rows, :] * shift_k(x, -1)
+                    + coupling[3, rows, :] * shift_k(x, 1)
+                )
+
+            def near_rest(rows, at, along_k):
+                ts = [
+                    along_k[v]
+                    + coupling[0, rows, :] * u[h, v, at - 1 : at + 7, :]
+                    + coupling[1, rows, :] * u[h, v, at + 1 : at + 9, :]
+                    for v in range(V)
+                ]
+                parity = (
+                    lax.broadcasted_iota(i32, (8, NK), 0) + lax.broadcasted_iota(i32, (8, NK), 1) + h
+                ) % 2
+                update = (frozen[rows, :] < 0.5) & (parity == 0)
+                for v in range(V):
+                    u[1 - h, v, at : at + 8, :] = jnp.where(
+                        update, apply(rows, ts, v), u[h, v, at : at + 8, :]
+                    )
+
+            def off_k(v, rows, at):
+                x = u[h, v, at : at + 8, :]
+                along = sum(a * shift_k(x, o) for o, a in zip(upwind_offsets, upwind_weights))
+                return source[v, rows, :] - coupling[1, rows, :] * along
+
+            def off_rest(rows, at, along_k):
+                ts = []
+                for v in range(V):
+                    along = sum(
+                        a * u[h, v, at + o : at + o + 8, :]
+                        for o, a in zip(upwind_offsets, upwind_weights)
+                    )
+                    ts.append(along_k[v] - coupling[0, rows, :] * along)
+                update = frozen[rows, :] < 0.5
+                for v in range(V):
+                    old = u[h, v, at : at + 8, :]
+                    u[1 - h, v, at : at + 8, :] = jnp.where(update, old + apply(rows, ts, v), old)
+
+            def before(of_k, rest):
+                for t in range(4):
+                    rows, at = slice(8 * t, 8 * t + 8), TOP + 8 * t
+                    along_k = [of_k(v, rows, at) for v in range(V)]
+                    if t in (1, 2):
+                        rest(rows, at, along_k)
+                    else:
+                        for v in range(V):
+                            part[v, rows, :] = along_k[v]
+
+            def after(rest):
+                for t in (0, 3):
+                    rows, at = slice(8 * t, 8 * t + 8), TOP + 8 * t
+                    rest(rows, at, [part[v, rows, :] for v in range(V)])
+
             @pl.when(is_near)
             def _():
-                for t in range(4):
-                    rows = slice(8 * t, 8 * t + 8)
-                    for v in range(V):
-                        x = u[h, v, TOP + 8 * t : TOP + 8 * t + 8, :]
-                        part[v, rows, :] = (
-                            source[v, rows, :]
-                            + coupling[2, rows, :] * shift_k(x, -1)
-                            + coupling[3, rows, :] * shift_k(x, 1)
-                        )
+                before(near_k, near_rest)
 
             @pl.when(jnp.logical_not(is_near))
             def _():
-                for t in range(4):
-                    rows = slice(8 * t, 8 * t + 8)
-                    for v in range(V):
-                        x = u[h, v, TOP + 8 * t : TOP + 8 * t + 8, :]
-                        along = sum(a * shift_k(x, o) for o, a in zip(upwind_offsets, upwind_weights))
-                        part[v, rows, :] = source[v, rows, :] - coupling[1, rows, :] * along
+                before(off_k, off_rest)
 
             @pl.when(has_low)
             def _():
@@ -235,45 +347,13 @@
                 for v in range(V):
                     u[h, v, TOP + NJ : TOP + NJ + 3, :] = hrecv[n, 1, 3 * v : 3 * v + 3, :]
 
-            def apply(rows, ts, v):
-                return sum(inverse[v, w, rows, :] * ts[w] for w in range(V))
-
             @pl.when(is_near)
             def _():
-                for t in range(4):
-                    rows = slice(8 * t, 8 * t + 8)
-                    at = TOP + 8 * t
-                    ts = [
-                        part[v, rows, :]
-                        + coupling[0, rows, :] * u[h, v, at - 1 : at + 7, :]
-                        + coupling[1, rows, :] * u[h, v, at + 1 : at + 9, :]
-                        for v in range(V)
-                    ]
-                    parity = (
-                        lax.broadcasted_iota(i32, (8, NK), 0) + lax.broadcasted_iota(i32, (8, NK), 1) + h
-                    ) % 2
-                    update = (frozen[rows, :] < 0.5) & (parity == 0)
-                    for v in range(V):
-                        u[1 - h, v, at : at + 8, :] = jnp.where(
-                            update, apply(rows, ts, v), u[h, v, at : at + 8, :]
-                        )
+                after(near_rest)
 
             @pl.when(jnp.logical_not(is_near))
             def _():
-                for t in range(4):
-                    rows = slice(8 * t, 8 * t + 8)
-                    at = TOP + 8 * t
-                    ts = []
-                    for v in range(V):
-                        along = sum(
-                            a * u[h, v, at + o : at + o + 8, :]
-                            for o, a in zip(upwind_offsets, upwind_weights)
-                        )
-                        ts.append(part[v, rows, :] - coupling[0, rows, :] * along)
-                    update = frozen[rows, :] < 0.5
-                    for v in range(V):
-                        old = u[h, v, at : at + 8, :]
-                        u[1 - h, v, at : at + 8, :] = jnp.where(update, old + apply(rows, ts, v), old)
+                after(off_rest)
 
             @pl.when(has_low)
             def _():
@@ -287,21 +367,30 @@
 
         lax.fori_loop(0, 2, half, 0)
 
-    for v in range(V):
-        out[v] = u[0, v, TOP : TOP + NJ, :]
+    store = pltpu.make_async_copy(block_rows(u), out, in_sem.at[0])
+    store.start()
+    store.wait()
 
 
 def on_device(field, source, block_inverse, coupling, donor_base, donor_weight, receiver_cell):
     blocks = donor_base.shape[2]
-    vmem = pl.BlockSpec(memory_space=pltpu.VMEM)
+    hbm = pl.BlockSpec(memory_space=pl.ANY)
     result = pl.pallas_call(
         functools.partial(kernel, blocks),
         out_shape=jax.ShapeDtypeStruct((V, NJ, NK), f32),
-        in_specs=[vmem] * 7,
-        out_specs=vmem,
+        in_specs=[hbm] * 7,
+        out_specs=hbm,
         scratch_shapes=[
+            pltpu.VMEM((V, NJ, NK), f32),
+            pltpu.VMEM((V, V, NJ, NK), f32),
+            pltpu.VMEM((4, NJ, NK), f32),
+            pltpu.VMEM((blocks, S), i32),
+            pltpu.VMEM((4, blocks, S), f32),
+            pltpu.VMEM((blocks, S), i32),
             pltpu.VMEM((2, V, TOP + NJ + 8, NK), f32),
-            pltpu.VMEM((640, NK), bf16),
+            pltpu.VMEM((960, NK // 2), bf16),
+            pltpu.VMEM((blocks, NK // 2, S), bf16),
+            pltpu.VMEM((blocks, 3, NJ, S), f32),
             pltpu.VMEM((blocks, 8, S), f32),
             pltpu.VMEM((ITERS, blocks, 8, S), f32),
             pltpu.VMEM((320, NK), f32),
@@ -313,6 +402,7 @@
             pltpu.SemaphoreType.DMA((ITERS, blocks // G)),
             pltpu.SemaphoreType.DMA((2,)),
             pltpu.SemaphoreType.DMA((2 * ITERS, 2)),
+            pltpu.SemaphoreType.DMA((7,)),
         ],
         compiler_params=pltpu.CompilerParams(
             collective_id=0, has_side_effects=True, vmem_limit_bytes=48 * 2**20

time: 142 us -> 130 us (0.915)
  Pallas kernels: 134 us -> 121 us
    pallas_call x1, Pallas kernels: 134 us -> 121 us  [on_device(): pl.pallas_call(functools.partial(kernel, blocks), out_shape=jax.ShapeDtyp...]
where the time goes in v2:
time: 130 us; the launch traced here: 129 us
  Pallas kernels  121 us (93%)
  local copies, waits for them, and re-layouts  7.68 us (6%)
    pallas_call x1, Pallas kernels, on_device(): pl.pallas_call(functools.partial(kernel, blocks), out_shape=jax.ShapeDtyp...  121 us
    unnamed x15, local copies, waits for them, and re-layouts  7.68 us

profile of v2, /device:TPU:32, one launch (start us, length us, event | category | flops | bytes accessed | tf_op | source)
XLA Modules:
  0.0 129.2 jit_solution(3295974136643660681)
XLA Ops:
  0.0 0.0 copy-start
  0.0 1.4 %copy-done = f32[1,1,5,5,32,512]{5,4,3,2,1,0:T(8,128)S(1)} copy-done((f32[1,1,5,5,32,512]{5,4,3,2,1,0:T(8,128)S(1)}, f32[1,1,5,5,32,512]{5,4,3,2,1,0:T(8,128)}, u32[]{:S(2)}) %copy-start) | copy-done | bytes 1638424
  1.4 0.0 copy-start.1
  1.4 1.0 copy-done.1
  2.4 0.0 copy-start.2
  2.4 1.0 copy-done.2
  3.4 0.0 copy-start.3
  3.4 0.9 copy-done.3
  4.3 0.0 copy-start.4
  4.3 0.9 copy-done.4
  5.3 0.0 copy-start.5
  5.3 0.8 copy-done.5
  6.1 0.0 copy-start.6
  6.1 0.8 copy-done.6
  7.0 121.5 %shard_map.73 = f32[5,32,512]{2,1,0:T(8,128)S(1)} custom-call(f32[5,32,512]{2,1,0:T(8,128)S(1)} %bitcast.10, f32[5,32,512]{2,1,0:T(8,128)S(1)} %bitcast.11, f32[5,5,32,512]{3,2,1,0:T(8,128)S(1)} %bitcast.8, f32[4,32,512]{2,1,0:T(8,128)S(1)} %bitcast.12, s32[64,256]{1,0:T(8,128)S(1)} %bitcast.14, f32[4,64,256]{2,1,0:T(8,128)S(1)} %bitcast.13, ...), custom_call_target="tpu_custom_call" | custom-call | tf_op jit(solution)/shard_map/pallas_call | solution.py:378
  128.4 0.7 copy.9
Async XLA Ops:
  0.0 1.4 %copy-start = (f32[1,1,5,5,32,512]{5,4,3,2,1,0:T(8,128)S(1)}, f32[1,1,5,5,32,512]{5,4,3,2,1,0:T(8,128)}, u32[]{:S(2)}) copy-start(f32[1,1,5,5,32,512]{5,4,3,2,1,0:T(8,128)} %param.9) | copy-start | bytes 4915204
  1.4 1.0 copy-start.1
  2.4 1.0 copy-start.2
  3.4 0.9 copy-start.3
  4.3 0.9 copy-start.4
  5.3 0.8 copy-start.5
  6.1 0.8 copy-start.6

commit v3 on v2

v3 whole, which is shorter than its diff:
```python
import functools

import jax
import jax.numpy as jnp
from jax import lax
from jax.experimental import pallas as pl
from jax.experimental.pallas import tpu as pltpu
from jax.sharding import PartitionSpec as P

ITERS = 4
V = 5
NJ = 32
NK = 512
S = 256
TOP = 16
G = 8

upwind_offsets = (-3, -2, -1, 0, 1, 2)
upwind_weights = (-2.0 / 60.0, 15.0 / 60.0, -60.0 / 60.0, 20.0 / 60.0, 30.0 / 60.0, -3.0 / 60.0)

f32, bf16, i32 = jnp.float32, jnp.bfloat16, jnp.int32
MESH = pl.DeviceIdType.MESH


def shift_k(x, o):
    if o == 0:
        return x
    n = x.shape[1]
    col = lax.broadcasted_iota(i32, x.shape, 1)
    rolled = pltpu.roll(x, (-o) % n, axis=1)
    keep = (col + o >= 0) & (col + o < n)
    return jnp.where(keep, rolled, 0.0)


def split(x):
    hi = x.astype(bf16)
    return hi, (x - hi.astype(f32)).astype(bf16)


def make_table(u, tab):
    for v in range(V):
        hl = jnp.concatenate(split(u[0, v, TOP : TOP + NJ, :]), axis=0)
        for e in range(2):
            pick = jnp.where(
                lax.broadcasted_iota(i32, (NK, NK // 2), 0)
                == 2 * lax.broadcasted_iota(i32, (NK, NK // 2), 1) + e,
                1.0,
                0.0,
            ).astype(bf16)
            t = jnp.dot(hl, pick, preferred_element_type=f32)
            parts = [(e, t)]
            if e == 0:
                first = jnp.concatenate([t[1:, :1], jnp.zeros((1, 1), f32)], axis=0)
                parts.append((2, jnp.concatenate([t[:, 1:], first], axis=1)))
            for o, p in parts:
                p = p.astype(bf16)
                tab[pl.ds(160 * o + 32 * v, 32), :] = p[:32]
                tab[pl.ds(480 + 160 * o + 32 * v, 32), :] = p[32:]


def one_hot(base):
    k = (base & (NK - 1)) >> 1
    return jnp.where(lax.broadcasted_iota(i32, (NK // 2, S), 0) == k, 1.0, 0.0).astype(bf16)


def patterns(base, w):
    even = (base & 1) == 0
    row = lax.broadcasted_iota(i32, (NJ, S), 0)
    here, below = row == (base >> 9), row == (base >> 9) + 1
    zero = jnp.zeros_like(w[0])

    def spread(x, y):
        return jnp.where(here, x, jnp.where(below, y, 0.0))

    return (
        spread(jnp.where(even, w[0], zero), jnp.where(even, w[2], zero)),
        spread(jnp.where(even, w[1], w[0]), jnp.where(even, w[3], w[2])),
        spread(jnp.where(even, zero, w[1]), jnp.where(even, zero, w[3])),
    )


def interpolate(tab, hot, ps):
    g = jnp.dot(tab[...], hot, preferred_element_type=f32)
    rows = []
    for v in range(V):
        total = None
        for o in range(3):
            at = 160 * o + 32 * v
            term = (g[at : at + 32] + g[480 + at : 512 + at]) * ps[o]
            total = term if total is None else total + term
        rows.append(jnp.sum(total, axis=0, keepdims=True))
    return jnp.concatenate(rows + [jnp.zeros((3, S), f32)], axis=0)


def kernel(
    blocks,
    field_hbm, source_hbm, inverse_hbm, coupling_hbm, base_hbm, weight_hbm, cell_hbm,
    out,
    source, inverse, coupling, base, weight, cell,
    u, tab, hots, pats, send, recv, acc, frozen, part,
    down_out, up_out, down_in, up_in, const_down_out, const_up_out, const_down_in, const_up_in,
    send_sem, recv_sem, hsend_sem, hrecv_sem, in_sem,
):
    g = lax.axis_index("group")
    b = lax.axis_index("blk")
    groups = blocks // G
    mine, within = b // G, b % G
    other = 1 - g
    is_near = g == 0
    has_low, has_high = b > 0, b < blocks - 1

    def block_rows(ref):
        return ref.at[0, :, pl.ds(TOP, NJ), :]

    loads = [
        pltpu.make_async_copy(a, c, in_sem.at[n])
        for n, (a, c) in enumerate(
            (
                (field_hbm, block_rows(u)),
                (base_hbm, base),
                (weight_hbm, weight),
                (cell_hbm, cell),
                (source_hbm, source.at[:, pl.ds(8, NJ), :]),
                (coupling_hbm, coupling.at[:, pl.ds(8, NJ), :]),
                (inverse_hbm, inverse.at[:, :, pl.ds(8, NJ), :]),
            )
        )
    ]
    for load in loads:
        load.start()

    barrier = pltpu.get_barrier_semaphore()

    def greet(d, c):
        pl.semaphore_signal(barrier, inc=1, device_id=(other, d), device_id_type=MESH)
        return c

    lax.fori_loop(0, blocks, greet, 0)

    for d in ((b + blocks - 1) % blocks, (b + 1) % blocks):
        pl.semaphore_signal(barrier, inc=1, device_id=(g, d), device_id_type=MESH)

    edge_tiles = (slice(0, 8), slice(8 + NJ, 16 + NJ))
    for v in range(V):
        u[0, v, 0:TOP, :] = jnp.zeros((TOP, NK), f32)
        u[0, v, TOP + NJ : 2 * TOP + NJ, :] = jnp.zeros((TOP, NK), f32)
    constants = (
        [(source, (v,)) for v in range(V)]
        + [(inverse, (v, w)) for v in range(V) for w in range(V)]
        + [(coupling, (n,)) for n in range(4)]
    )
    for ref, at in constants + [(frozen, ())]:
        for rows in edge_tiles:
            ref[at + (rows, slice(None))] = jnp.zeros((8, NK), f32)
    for ref in (down_out, up_out, const_down_out, const_up_out):
        ref[...] = jnp.zeros_like(ref)

    for load in loads[:3]:
        load.wait()

    def message(it, i, d):
        return pltpu.make_async_remote_copy(
            src_ref=send.at[d],
            dst_ref=recv.at[it, b],
            send_sem=send_sem,
            recv_sem=recv_sem.at[it, i],
            device_id=(other, d),
            device_id_type=MESH,
        )

    def ship(src, dst, n, direction, slot):
        return pltpu.make_async_remote_copy(
            src_ref=src,
            dst_ref=dst,
            send_sem=hsend_sem.at[n],
            recv_sem=hrecv_sem.at[slot, n],
            device_id=(g, b + direction),
            device_id_type=MESH,
        )

    def edges(it, rows):
        return (
            ship(down_out, down_in.at[it], 0, -1, it),
            ship(up_out.at[pl.ds(0, rows)], up_in.at[it, pl.ds(0, rows)], 1, 1, it),
        )

    def const_edges():
        return (
            ship(const_down_out, const_down_in, 2, -1, 0),
            ship(const_up_out, const_up_in, 3, 1, 0),
        )

    def sweep(it, opening):
        make_table(u, tab)

        def gather_group(i, c):
            dg = (mine + i) % groups
            first = pl.multiple_of(dg * G, G)
            if opening:
                bases = base[pl.ds(first, G), :]
                ws = [weight[q, pl.ds(first, G), :] for q in range(4)]
            for q in range(G):
                if opening:
                    hot = one_hot(bases[q : q + 1])
                    ps = patterns(bases[q : q + 1], [w[q : q + 1] for w in ws])
                    hots[first + q] = hot
                    for o in range(3):
                        pats[first + q, o] = ps[o]
                else:
                    hot = hots[first + q]
                    ps = [pats[first + q, o] for o in range(3)]
                send[first + q] = interpolate(tab, hot, ps)
            if opening:

                @pl.when(i == 0)
                def _():
                    pl.semaphore_wait(barrier, blocks + 2)

            for q in range(G):
                message(it, i, first + (within + q) % G).start()
            return c

        lax.fori_loop(0, groups, gather_group, 0)

        acc[...] = jnp.zeros_like(acc)
        if opening:
            frozen[8 : 8 + NJ, :] = jnp.zeros((NJ, NK), f32)
            for load in loads[3:]:
                load.wait()
            for n, (ref, at) in enumerate(constants):
                const_down_out[2 * n : 2 * n + 2, :] = ref[at + (slice(8, 10), slice(None))]
                const_up_out[3 * n : 3 * n + 3, :] = ref[at + (slice(5 + NJ, 8 + NJ), slice(None))]
            const_down, const_up = const_edges()

            @pl.when(has_low)
            def _():
                const_down.start()

            @pl.when(has_high)
            def _():
                const_up.start()


        def scatter_group(i, c):
            sg = (mine + groups - i) % groups
            first = pl.multiple_of(sg * G, G)
            pltpu.make_async_copy(
                recv.at[it, pl.ds(first, G)], recv.at[it, pl.ds(first, G)], recv_sem.at[it, i]
            ).wait()
            cells = cell[pl.ds(first, G), :]
            left, right = [], []
            for q in range(G):
                r = cells[q : q + 1]
                hit = lax.broadcasted_iota(i32, (NJ, S), 0) == (r >> 9)
                val = recv[it, first + q]
                hi = val.astype(bf16).astype(f32)
                rows = [
                    jnp.where(hit, t[v : v + 1], 0.0) for t in (hi, val - hi) for v in range(V)
                ]
                if opening:
                    rows.append(jnp.where(hit, 1.0, 0.0))
                left.append(jnp.concatenate(rows, axis=0).astype(bf16))
                right.append(
                    jnp.where(
                        lax.broadcasted_iota(i32, (NK, S), 0) == (r & (NK - 1)), 1.0, 0.0
                    ).astype(bf16)
                )
            p = lax.dot_general(
                jnp.concatenate(left, axis=1),
                jnp.concatenate(right, axis=1),
                (((1,), (1,)), ((), ())),
                preferred_element_type=f32,
            )
            acc[...] += p[:320]
            if opening:
                frozen[8 : 8 + NJ, :] += p[320:]
            return c

        lax.fori_loop(0, groups, scatter_group, 0)

        pltpu.make_async_copy(send, send, send_sem).wait()

        fixed = frozen[8 : 8 + NJ, :] > 0.5
        for v in range(V):
            placed = acc[32 * v : 32 * v + 32] + acc[160 + 32 * v : 192 + 32 * v]
            u[0, v, TOP : TOP + NJ, :] = jnp.where(fixed, placed, u[0, v, TOP : TOP + NJ, :])

        for v in range(V):
            down_out[4 * v : 4 * v + 4, :] = u[0, v, TOP : TOP + 4, :]
            up_out[6 * v : 6 * v + 6, :] = u[0, v, TOP + NJ - 6 : TOP + NJ, :]
        if opening:
            down_out[20:22, :] = frozen[8:10, :]
            up_out[30:33, :] = frozen[5 + NJ : 8 + NJ, :]
        down, up = edges(it, 40 if opening else 32)

        @pl.when(has_low)
        def _():
            down.start()

        @pl.when(has_high)
        def _():
            up.start()

        def apply(rows, ts, v):
            return sum(inverse[v, w, rows, :] * ts[w] for w in range(V))

        def near_k(h, v, rows, at):
            x = u[h, v, at : at + 8, :]
            return (
                source[v, rows, :]
                + coupling[2, rows, :] * shift_k(x, -1)
                + coupling[3, rows, :] * shift_k(x, 1)
            )

        def near_rest(h, rows, at, along_k):
            ts = [
                along_k[v]
                + coupling[0, rows, :] * u[h, v, at - 1 : at + 7, :]
                + coupling[1, rows, :] * u[h, v, at + 1 : at + 9, :]
                for v in range(V)
            ]
            parity = (
                lax.broadcasted_iota(i32, (8, NK), 0) + lax.broadcasted_iota(i32, (8, NK), 1)
            ) & 1
            update = (frozen[rows, :] < 0.5) & (parity == h)
            for v in range(V):
                u[1 - h, v, at : at + 8, :] = jnp.where(
                    update, apply(rows, ts, v), u[h, v, at : at + 8, :]
                )

        def off_k(h, v, rows, at):
            x = u[h, v, at : at + 8, :]
            along = sum(a * shift_k(x, o) for o, a in zip(upwind_offsets, upwind_weights))
            return source[v, rows, :] - coupling[1, rows, :] * along

        def off_rest(h, rows, at, along_k):
            ts = []
            for v in range(V):
                along = sum(
                    a * u[h, v, at + o : at + o + 8, :]
                    for o, a in zip(upwind_offsets, upwind_weights)
                )
                ts.append(along_k[v] - coupling[0, rows, :] * along)
            update = frozen[rows, :] < 0.5
            for v in range(V):
                old = u[h, v, at : at + 8, :]
                u[1 - h, v, at : at + 8, :] = jnp.where(update, old + apply(rows, ts, v), old)

        def tile(t):
            return slice(8 * t + 8, 8 * t + 16), TOP + 8 * t

        def before(of_k, rest):
            for t in range(4):
                rows, at = tile(t)
                along_k = [of_k(0, v, rows, at) for v in range(V)]
                if t in (1, 2):
                    rest(0, rows, at, along_k)
                else:
                    for v in range(V):
                        part[v, 8 * t : 8 * t + 8, :] = along_k[v]

        def after(of_k, rest):
            for t in (0, 3):
                rows, at = tile(t)
                rest(0, rows, at, [part[v, 8 * t : 8 * t + 8, :] for v in range(V)])
            for t in (-1, 4):
                rows, at = tile(t)
                rest(0, rows, at, [of_k(0, v, rows, at) for v in range(V)])
            for t in range(4):
                rows, at = tile(t)
                rest(1, rows, at, [of_k(1, v, rows, at) for v in range(V)])

        @pl.when(is_near)
        def _():
            before(near_k, near_rest)

        @pl.when(jnp.logical_not(is_near))
        def _():
            before(off_k, off_rest)

        @pl.when(has_low)
        def _():
            up.wait_recv()
            for v in range(V):
                u[0, v, TOP - 6 : TOP, :] = up_in[it, 6 * v : 6 * v + 6, :]
            if opening:
                frozen[5:8, :] = up_in[it, 30:33, :]
                const_up.wait_recv()
                for n, (ref, at) in enumerate(constants):
                    ref[at + (slice(5, 8), slice(None))] = const_up_in[3 * n : 3 * n + 3, :]

        @pl.when(has_high)
        def _():
            down.wait_recv()
            for v in range(V):
                u[0, v, TOP + NJ : TOP + NJ + 4, :] = down_in[it, 4 * v : 4 * v + 4, :]
            if opening:
                frozen[8 + NJ : 10 + NJ, :] = down_in[it, 20:22, :]
                const_down.wait_recv()
                for n, (ref, at) in enumerate(constants):
                    ref[at + (slice(8 + NJ, 10 + NJ), slice(None))] = const_down_in[2 * n : 2 * n + 2, :]

        @pl.when(is_near)
        def _():
            after(near_k, near_rest)

        @pl.when(jnp.logical_not(is_near))
        def _():
            after(off_k, off_rest)

        @pl.when(has_low)
        def _():
            down.wait_send()
            if opening:
                const_down.wait_send()

        @pl.when(has_high)
        def _():
            up.wait_send()
            if opening:
                const_up.wait_send()

    sweep(0, True)

    def later(it, c):
        sweep(it, False)
        return c

    lax.fori_loop(1, ITERS, later, 0)

    store = pltpu.make_async_copy(block_rows(u), out, in_sem.at[0])
    store.start()
    store.wait()


def on_device(field, source, block_inverse, coupling, donor_base, donor_weight, receiver_cell):
    blocks = donor_base.shape[2]
    hbm = pl.BlockSpec(memory_space=pl.ANY)
    result = pl.pallas_call(
        functools.partial(kernel, blocks),
        out_shape=jax.ShapeDtypeStruct((V, NJ, NK), f32),
        in_specs=[hbm] * 7,
        out_specs=hbm,
        scratch_shapes=[
            pltpu.VMEM((V, NJ + 16, NK), f32),
            pltpu.VMEM((V, V, NJ + 16, NK), f32),
            pltpu.VMEM((4, NJ + 16, NK), f32),
            pltpu.VMEM((blocks, S), i32),
            pltpu.VMEM((4, blocks, S), f32),
            pltpu.VMEM((blocks, S), i32),
            pltpu.VMEM((2, V, 2 * TOP + NJ, NK), f32),
            pltpu.VMEM((960, NK // 2), bf16),
            pltpu.VMEM((blocks, NK // 2, S), bf16),
            pltpu.VMEM((blocks, 3, NJ, S), f32),
            pltpu.VMEM((blocks, 8, S), f32),
            pltpu.VMEM((ITERS, blocks, 8, S), f32),
            pltpu.VMEM((320, NK), f32),
            pltpu.VMEM((NJ + 16, NK), f32),
            pltpu.VMEM((V, NJ, NK), f32),
            pltpu.VMEM((24, NK), f32),
            pltpu.VMEM((40, NK), f32),
            pltpu.VMEM((ITERS, 24, NK), f32),
            pltpu.VMEM((ITERS, 40, NK), f32),
            pltpu.VMEM((72, NK), f32),
            pltpu.VMEM((104, NK), f32),
            pltpu.VMEM((72, NK), f32),
            pltpu.VMEM((104, NK), f32),
            pltpu.SemaphoreType.DMA,
            pltpu.SemaphoreType.DMA((ITERS, blocks // G)),
            pltpu.SemaphoreType.DMA((4,)),
            pltpu.SemaphoreType.DMA((ITERS, 4)),
            pltpu.SemaphoreType.DMA((7,)),
        ],
        compiler_params=pltpu.CompilerParams(
            collective_id=0, has_side_effects=True, vmem_limit_bytes=60 * 2**20
        ),
    )(
        field[0, 0],
        source[0, 0],
        block_inverse[0, 0],
        coupling[0, 0],
        donor_base[0, 0],
        donor_weight[0, 0],
        receiver_cell[0, 0],
    )
    return result[None, None]


def solution(mesh):
    in_specs = (
        P("group", "blk", None, None, None),
        P("group", "blk", None, None, None),
        P("group", "blk", None, None, None, None),
        P("group", "blk", None, None, None),
        P("group", "blk", None, None),
        P("group", "blk", None, None, None),
        P("group", "blk", None, None),
    )
    out_specs = P("group", "blk", None, None, None)
    return jax.shard_map(
        on_device, mesh=mesh, in_specs=in_specs, out_specs=out_specs, check_vma=False
    )
```

time: 130 us -> 108 us (0.83)
  Pallas kernels: 121 us -> 105 us
  local copies, waits for them, and re-layouts: 7.68 us -> 1.72 us
    pallas_call x1, Pallas kernels: 121 us -> 105 us  [on_device(): pl.pallas_call(functools.partial(kernel, blocks), out_shape=jax.ShapeDtyp...]
    unnamed x15 -> x1, local copies, waits for them, and re-layouts: 7.68 us -> 1.72 us
where the time goes in v3:
time: 108 us; the launch traced here: 107 us
  Pallas kernels  105 us (97%)
  local copies, waits for them, and re-layouts  1.72 us (2%)
    pallas_call x1, Pallas kernels, on_device(): pl.pallas_call(functools.partial(kernel, blocks), out_shape=jax.ShapeDtyp...  105 us

profile of v3, /device:TPU:32, one launch (start us, length us, event | category | flops | bytes accessed | tf_op | source)
XLA Modules:
  0.0 106.9 jit_solution(4787764554812208733)
XLA Ops:
  0.0 105.1 %shard_map.73 = f32[5,32,512]{2,1,0:T(8,128)} custom-call(f32[5,32,512]{2,1,0:T(8,128)} %bitcast.10, f32[5,32,512]{2,1,0:T(8,128)} %bitcast.11, f32[5,5,32,512]{3,2,1,0:T(8,128)} %bitcast.8, f32[4,32,512]{2,1,0:T(8,128)} %bitcast.12, s32[64,256]{1,0:T(8,128)} %bitcast.14, f32[4,64,256]{2,1,0:T(8,128)} %bitcast.13, s32[64,256]{1,0:T(8,128)} %bitcast.15), custom_call_target="tpu_custom_call" | custom-call | tf_op jit(solution)/shard_map/pallas_call | solution.py:439
  105.2 1.7 %copy.9 = f32[1,1,5,32,512]{4,3,2,1,0:T(8,128)} copy(f32[1,1,5,32,512]{4,3,2,1,0:T(8,128)} %bitcast.9) | data formatting | bytes 655360

commit v4 on v3

--- a/solution.py
+++ b/solution.py
@@ -19,6 +19,8 @@
 upwind_weights = (-2.0 / 60.0, 15.0 / 60.0, -60.0 / 60.0, 20.0 / 60.0, 30.0 / 60.0, -3.0 / 60.0)
 
 f32, bf16, i32 = jnp.float32, jnp.bfloat16, jnp.int32
+f8 = jnp.float8_e4m3fn
+LIFT = 65536.0
 MESH = pl.DeviceIdType.MESH
 
 
@@ -37,30 +39,35 @@
     return hi, (x - hi.astype(f32)).astype(bf16)
 
 
-def make_table(u, tab):
-    for v in range(V):
-        hl = jnp.concatenate(split(u[0, v, TOP : TOP + NJ, :]), axis=0)
-        for e in range(2):
-            pick = jnp.where(
-                lax.broadcasted_iota(i32, (NK, NK // 2), 0)
-                == 2 * lax.broadcasted_iota(i32, (NK, NK // 2), 1) + e,
-                1.0,
-                0.0,
-            ).astype(bf16)
-            t = jnp.dot(hl, pick, preferred_element_type=f32)
-            parts = [(e, t)]
-            if e == 0:
-                first = jnp.concatenate([t[1:, :1], jnp.zeros((1, 1), f32)], axis=0)
-                parts.append((2, jnp.concatenate([t[:, 1:], first], axis=1)))
-            for o, p in parts:
-                p = p.astype(bf16)
-                tab[pl.ds(160 * o + 32 * v, 32), :] = p[:32]
-                tab[pl.ds(480 + 160 * o + 32 * v, 32), :] = p[32:]
+def largest(x):
+    m = jnp.max(jnp.max(jnp.abs(x), axis=1, keepdims=True), axis=0, keepdims=True)
+    return jnp.maximum(m, 1e-30)
+
+
+def swap_columns(inverse):
+    a = lax.broadcasted_iota(i32, (NK, NK), 1 if inverse else 0)
+    c = lax.broadcasted_iota(i32, (NK, NK), 0 if inverse else 1)
+    return jnp.where(a == 2 * (c & (NK // 2 - 1)) + (c >> 8), 1.0, 0.0).astype(bf16)
+
+
+def make_table(u, tab, tab8, pick):
+    a = jnp.concatenate([u[0, v, TOP : TOP + NJ, :] for v in range(V)], axis=0)
+    m = largest(a)
+    t = jnp.dot(
+        jnp.concatenate(split(a * (LIFT / m)), axis=0), pick[...], preferred_element_type=f32
+    )
+    t0, t1 = t[:, : NK // 2], t[:, NK // 2 :]
+    first = jnp.concatenate([t0[1:, :1], jnp.zeros((1, 1), f32)], axis=0)
+    t2 = jnp.concatenate([t0[:, 1:], first], axis=1)
+    for o, p in enumerate((t0, t1, t2)):
+        tab[pl.ds(160 * o, 160), :] = p[:160].astype(bf16)
+        tab8[pl.ds(160 * o, 160), :] = p[160:].astype(f8)
+    return m * (1.0 / LIFT)
 
 
 def one_hot(base):
     k = (base & (NK - 1)) >> 1
-    return jnp.where(lax.broadcasted_iota(i32, (NK // 2, S), 0) == k, 1.0, 0.0).astype(bf16)
+    return jnp.where(lax.broadcasted_iota(i32, (NK // 2, S), 0) == k, 1.0, 0.0)
 
 
 def patterns(base, w):
@@ -79,17 +86,23 @@
     )
 
 
-def interpolate(tab, hot, ps):
-    g = jnp.dot(tab[...], hot, preferred_element_type=f32)
+def interpolate(tab, tab8, hot, hot8, ps, undo):
+    high = jnp.dot(tab[...], hot, preferred_element_type=f32)
+    low = jnp.dot(tab8[...], hot8, preferred_element_type=f32)
     rows = []
     for v in range(V):
         total = None
         for o in range(3):
             at = 160 * o + 32 * v
-            term = (g[at : at + 32] + g[480 + at : 512 + at]) * ps[o]
+            term = (high[at : at + 32] + low[at : at + 32]) * ps[o]
             total = term if total is None else total + term
         rows.append(jnp.sum(total, axis=0, keepdims=True))
-    return jnp.concatenate(rows + [jnp.zeros((3, S), f32)], axis=0)
+    return jnp.concatenate(rows + [jnp.zeros((3, S), f32)], axis=0) * undo
+
+
+def rows_of(half):
+    r = lax.broadcasted_iota(i32, (16, S), 0)
+    return r + 8 if half else jnp.where(r < 8, r, r + 16)
 
 
 def kernel(
@@ -97,7 +110,8 @@
     field_hbm, source_hbm, inverse_hbm, coupling_hbm, base_hbm, weight_hbm, cell_hbm,
     out,
     source, inverse, coupling, base, weight, cell,
-    u, tab, hots, pats, send, recv, acc, frozen, part,
+    u, tab, tab8, pick, spread, hots, hots8, pats, cell_hots, cell_hots8,
+    send, recv, acc, marks, frozen, part,
     down_out, up_out, down_in, up_in, const_down_out, const_up_out, const_down_in, const_up_in,
     send_sem, recv_sem, hsend_sem, hrecv_sem, in_sem,
 ):
@@ -155,6 +169,9 @@
     for ref in (down_out, up_out, const_down_out, const_up_out):
         ref[...] = jnp.zeros_like(ref)
 
+    pick[...] = swap_columns(False)
+    spread[...] = swap_columns(True)
+
     for load in loads[:3]:
         load.wait()
 
@@ -191,7 +208,7 @@
         )
 
     def sweep(it, opening):
-        make_table(u, tab)
+        undo = make_table(u, tab, tab8, pick)
 
         def gather_group(i, c):
             dg = (mine + i) % groups
@@ -202,14 +219,16 @@
             for q in range(G):
                 if opening:
                     hot = one_hot(bases[q : q + 1])
+                    hot, hot8 = hot.astype(bf16), hot.astype(f8)
                     ps = patterns(bases[q : q + 1], [w[q : q + 1] for w in ws])
                     hots[first + q] = hot
+                    hots8[first + q] = hot8
                     for o in range(3):
                         pats[first + q, o] = ps[o]
                 else:
-                    hot = hots[first + q]
+                    hot, hot8 = hots[first + q], hots8[first + q]
                     ps = [pats[first + q, o] for o in range(3)]
-                send[first + q] = interpolate(tab, hot, ps)
+                send[first + q] = interpolate(tab, tab8, hot, hot8, ps, undo)
             if opening:
 
                 @pl.when(i == 0)
@@ -222,9 +241,7 @@
 
         lax.fori_loop(0, groups, gather_group, 0)
 
-        acc[...] = jnp.zeros_like(acc)
         if opening:
-            frozen[8 : 8 + NJ, :] = jnp.zeros((NJ, NK), f32)
             for load in loads[3:]:
                 load.wait()
             for n, (ref, at) in enumerate(constants):
@@ -241,49 +258,80 @@
                 const_up.start()
 
 
-        def scatter_group(i, c):
+        def scatter_group(i, c, half):
             sg = (mine + groups - i) % groups
             first = pl.multiple_of(sg * G, G)
-            pltpu.make_async_copy(
-                recv.at[it, pl.ds(first, G)], recv.at[it, pl.ds(first, G)], recv_sem.at[it, i]
-            ).wait()
+            if not half:
+                pltpu.make_async_copy(
+                    recv.at[it, pl.ds(first, G)], recv.at[it, pl.ds(first, G)], recv_sem.at[it, i]
+                ).wait()
             cells = cell[pl.ds(first, G), :]
-            left, right = [], []
+            slots = pl.ds(pl.multiple_of(first * S, S), G * S)
+            if opening and not half:
+                down_cells = jnp.transpose(cells.astype(f32)).astype(i32)
+                for q in range(G):
+                    hot = jnp.where(
+                        lax.broadcasted_iota(i32, (S, NK // 2), 1)
+                        == (down_cells[:, q : q + 1] & (NK - 1)) >> 1,
+                        1.0,
+                        0.0,
+                    )
+                    at = pl.ds(pl.multiple_of((first + q) * S, S), S)
+                    cell_hots[at, :] = hot.astype(bf16)
+                    cell_hots8[at, :] = hot.astype(f8)
+            vals = [recv[it, first + q] for q in range(G)]
+            m = largest(functools.reduce(jnp.maximum, [jnp.abs(x) for x in vals]))
+            scale = LIFT / m
+            highs, lows = [], []
             for q in range(G):
                 r = cells[q : q + 1]
-                hit = lax.broadcasted_iota(i32, (NJ, S), 0) == (r >> 9)
-                val = recv[it, first + q]
-                hi = val.astype(bf16).astype(f32)
-                rows = [
-                    jnp.where(hit, t[v : v + 1], 0.0) for t in (hi, val - hi) for v in range(V)
-                ]
+                hit = rows_of(half) == (r >> 9)
+                even = (r & 1) == 0
+                hits = (hit & even, hit & jnp.logical_not(even))
+                high = vals[q].astype(bf16).astype(f32)
+                low = (vals[q] - high) * scale
+                rows = [jnp.where(x, high[v : v + 1], 0.0) for x in hits for v in range(V)]
                 if opening:
-                    rows.append(jnp.where(hit, 1.0, 0.0))
-                left.append(jnp.concatenate(rows, axis=0).astype(bf16))
-                right.append(
-                    jnp.where(
-                        lax.broadcasted_iota(i32, (NK, S), 0) == (r & (NK - 1)), 1.0, 0.0
-                    ).astype(bf16)
-                )
-            p = lax.dot_general(
-                jnp.concatenate(left, axis=1),
-                jnp.concatenate(right, axis=1),
-                (((1,), (1,)), ((), ())),
-                preferred_element_type=f32,
+                    rows += [jnp.where(x, 1.0, 0.0) for x in hits]
+                highs.append(jnp.concatenate(rows, axis=0).astype(bf16))
+                rows = [jnp.where(x, low[v : v + 1], 0.0) for x in hits for v in range(V)]
+                lows.append(jnp.concatenate(rows, axis=0).astype(f8))
+            p = jnp.dot(
+                jnp.concatenate(highs, axis=1), cell_hots[slots, :], preferred_element_type=f32
             )
-            acc[...] += p[:320]
-            if opening:
-                frozen[8 : 8 + NJ, :] += p[320:]
+            acc[0] += p[:160]
+            if opening:
+                marks[...] += p[160:]
+            p = jnp.dot(
+                jnp.concatenate(lows, axis=1), cell_hots8[slots, :], preferred_element_type=f32
+            )
+            acc[1] += p * (m * (1.0 / LIFT))
             return c
 
-        lax.fori_loop(0, groups, scatter_group, 0)
-
-        pltpu.make_async_copy(send, send, send_sem).wait()
-
-        fixed = frozen[8 : 8 + NJ, :] > 0.5
-        for v in range(V):
-            placed = acc[32 * v : 32 * v + 32] + acc[160 + 32 * v : 192 + 32 * v]
-            u[0, v, TOP : TOP + NJ, :] = jnp.where(fixed, placed, u[0, v, TOP : TOP + NJ, :])
+        def interleave(even, odd):
+            pair = jnp.concatenate([even, odd], axis=1).astype(bf16)
+            return jnp.dot(pair, spread[...], preferred_element_type=f32)
+
+        def place(half):
+            acc[...] = jnp.zeros_like(acc)
+            if opening:
+                marks[...] = jnp.zeros_like(marks)
+            lax.fori_loop(0, groups, functools.partial(scatter_group, half=half), 0)
+            placed = interleave(acc[0, :80, :], acc[0, 80:, :]) + interleave(acc[1, :80, :], acc[1, 80:, :])
+            pieces = ((0, 8), (8, 16)) if half else ((0, 0), (8, 24))
+            if opening:
+                mark = interleave(marks[:16, :], marks[16:, :])
+            for n, j in pieces:
+                if opening:
+                    frozen[8 + j : 16 + j, :] = mark[n : n + 8]
+                fixed = frozen[8 + j : 16 + j, :] > 0.5
+                for v in range(V):
+                    at = TOP + j
+                    u[0, v, at : at + 8, :] = jnp.where(
+                        fixed, placed[16 * v + n : 16 * v + n + 8], u[0, v, at : at + 8, :]
+                    )
+
+        place(0)
 
         for v in range(V):
             down_out[4 * v : 4 * v + 4, :] = u[0, v, TOP : TOP + 4, :]
@@ -300,6 +348,10 @@
         @pl.when(has_high)
         def _():
             up.start()
+
+        place(1)
+
+        pltpu.make_async_copy(send, send, send_sem).wait()
 
         def apply(rows, ts, v):
             return sum(inverse[v, w, rows, :] * ts[w] for w in range(V))
@@ -449,12 +501,19 @@
             pltpu.VMEM((4, blocks, S), f32),
             pltpu.VMEM((blocks, S), i32),
             pltpu.VMEM((2, V, 2 * TOP + NJ, NK), f32),
-            pltpu.VMEM((960, NK // 2), bf16),
+            pltpu.VMEM((480, NK // 2), bf16),
+            pltpu.VMEM((480, NK // 2), f8),
+            pltpu.VMEM((NK, NK), bf16),
+            pltpu.VMEM((NK, NK), bf16),
             pltpu.VMEM((blocks, NK // 2, S), bf16),
+            pltpu.VMEM((blocks, NK // 2, S), f8),
             pltpu.VMEM((blocks, 3, NJ, S), f32),
+            pltpu.VMEM((blocks * S, NK // 2), bf16),
+            pltpu.VMEM((blocks * S, NK // 2), f8),
             pltpu.VMEM((blocks, 8, S), f32),
             pltpu.VMEM((ITERS, blocks, 8, S), f32),
-            pltpu.VMEM((320, NK), f32),
+            pltpu.VMEM((2, 160, NK // 2), f32),
+            pltpu.VMEM((32, NK // 2), f32),
             pltpu.VMEM((NJ + 16, NK), f32),
             pltpu.VMEM((V, NJ, NK), f32),
             pltpu.VMEM((24, NK), f32),

time: 108 us -> 101 us (0.935)
  the two profiles are of different devices: /device:TPU:32 before, /device:TPU:1 now
where the time goes in v4:
time: 101 us
  Pallas kernels  98.9 us (98%)
  local copies, waits for them, and re-layouts  1.72 us (2%)
    pallas_call x1, Pallas kernels, on_device(): pl.pallas_call(functools.partial(kernel, blocks), out_shape=jax.ShapeDtyp...  98.9 us

profile of v4, /device:TPU:1, one launch (start us, length us, event | category | flops | bytes accessed | tf_op | source)
XLA Modules:
  0.0 100.7 jit_solution(4361131760476459924)
XLA Ops:
  0.0 98.9 %shard_map.73 = f32[5,32,512]{2,1,0:T(8,128)} custom-call(f32[5,32,512]{2,1,0:T(8,128)} %bitcast.10, f32[5,32,512]{2,1,0:T(8,128)} %bitcast.11, f32[5,5,32,512]{3,2,1,0:T(8,128)} %bitcast.8, f32[4,32,512]{2,1,0:T(8,128)} %bitcast.12, s32[64,256]{1,0:T(8,128)} %bitcast.14, f32[4,64,256]{2,1,0:T(8,128)} %bitcast.13, s32[64,256]{1,0:T(8,128)} %bitcast.15), custom_call_target="tpu_custom_call" | custom-call | tf_op jit(solution)/shard_map/pallas_call | solution.py:491
  98.9 1.7 %copy.9 = f32[1,1,5,32,512]{4,3,2,1,0:T(8,128)} copy(f32[1,1,5,32,512]{4,3,2,1,0:T(8,128)} %bitcast.9) | data formatting | bytes 655360

commit v5 on v4

--- a/solution.py
+++ b/solution.py
@@ -175,6 +175,9 @@
     for load in loads[:3]:
         load.wait()
 
+    def far_first(turn):
+        return groups // 2 + ((turn + 1) // 2) * (1 - 2 * (turn % 2))
+
     def message(it, i, d):
         return pltpu.make_async_remote_copy(
             src_ref=send.at[d],
@@ -210,7 +213,8 @@
     def sweep(it, opening):
         undo = make_table(u, tab, tab8, pick)
 
-        def gather_group(i, c):
+        def gather_group(turn, c):
+            i = far_first(turn)
             dg = (mine + i) % groups
             first = pl.multiple_of(dg * G, G)
             if opening:
@@ -231,7 +235,7 @@
                 send[first + q] = interpolate(tab, tab8, hot, hot8, ps, undo)
             if opening:
 
-                @pl.when(i == 0)
+                @pl.when(turn == 0)
                 def _():
                     pl.semaphore_wait(barrier, blocks + 2)
 
@@ -258,7 +262,8 @@
                 const_up.start()
 
 
-        def scatter_group(i, c, half):
+        def scatter_group(turn, c, half):
+            i = far_first(turn)
             sg = (mine + groups - i) % groups
             first = pl.multiple_of(sg * G, G)
             if not half:
@@ -480,9 +485,8 @@
 
     lax.fori_loop(1, ITERS, later, 0)
 
-    store = pltpu.make_async_copy(block_rows(u), out, in_sem.at[0])
-    store.start()
-    store.wait()
+    for v in range(V):
+        out[v] = u[0, v, TOP : TOP + NJ, :]
 
 
 def on_device(field, source, block_inverse, coupling, donor_base, donor_weight, receiver_cell):
@@ -492,7 +496,7 @@
         functools.partial(kernel, blocks),
         out_shape=jax.ShapeDtypeStruct((V, NJ, NK), f32),
         in_specs=[hbm] * 7,
-        out_specs=hbm,
+        out_specs=pl.BlockSpec(memory_space=pltpu.VMEM),
         scratch_shapes=[
             pltpu.VMEM((V, NJ + 16, NK), f32),
             pltpu.VMEM((V, V, NJ + 16, NK), f32),
@@ -531,7 +535,7 @@
             pltpu.SemaphoreType.DMA((7,)),
         ],
         compiler_params=pltpu.CompilerParams(
-            collective_id=0, has_side_effects=True, vmem_limit_bytes=60 * 2**20
+            collective_id=0, has_side_effects=True, vmem_limit_bytes=63 * 2**20
         ),
     )(
         field[0, 0],

time: 101 us -> 97.5 us (0.965)
  the two profiles are of different devices: /device:TPU:1 before, /device:TPU:32 now
where the time goes in v5:
time: 97.5 us; the launch traced here: 95.8 us
  Pallas kernels  94.1 us (97%)
  local copies, waits for them, and re-layouts  1.72 us (2%)
    pallas_call x1, Pallas kernels, on_device(): pl.pallas_call(functools.partial(kernel, blocks), out_shape=jax.ShapeDtyp...  94.1 us

profile of v5, /device:TPU:32, one launch (start us, length us, event | category | flops | bytes accessed | tf_op | source)
XLA Modules:
  0.0 95.8 jit_solution(2885871141830306428)
XLA Ops:
  0.0 94.1 %shard_map.73 = f32[5,32,512]{2,1,0:T(8,128)} custom-call(f32[5,32,512]{2,1,0:T(8,128)} %bitcast.10, f32[5,32,512]{2,1,0:T(8,128)} %bitcast.11, f32[5,5,32,512]{3,2,1,0:T(8,128)} %bitcast.8, f32[4,32,512]{2,1,0:T(8,128)} %bitcast.12, s32[64,256]{1,0:T(8,128)} %bitcast.14, f32[4,64,256]{2,1,0:T(8,128)} %bitcast.13, s32[64,256]{1,0:T(8,128)} %bitcast.15), custom_call_target="tpu_custom_call" | custom-call | tf_op jit(solution)/shard_map/pallas_call | solution.py:495
  94.1 1.7 %copy.9 = f32[1,1,5,32,512]{4,3,2,1,0:T(8,128)} copy(f32[1,1,5,32,512]{4,3,2,1,0:T(8,128)} %bitcast.9) | data formatting | bytes 655360

commit v6 on v5

--- a/solution.py
+++ b/solution.py
@@ -118,7 +118,6 @@
     g = lax.axis_index("group")
     b = lax.axis_index("blk")
     groups = blocks // G
-    mine, within = b // G, b % G
     other = 1 - g
     is_near = g == 0
     has_low, has_high = b > 0, b < blocks - 1
@@ -175,16 +174,25 @@
     for load in loads[:3]:
         load.wait()
 
-    def far_first(turn):
-        return groups // 2 + ((turn + 1) // 2) * (1 - 2 * (turn % 2))
-
-    def message(it, i, d):
+    def far_first(n):
+        return 2 + ((n + 1) // 2) * (1 - 2 * (n % 2))
+
+    def partner(turn, q, sign):
+        dz, dy, dx = far_first(turn // 2), far_first(2 * (turn % 2) + q // 4), far_first(q % 4)
+        z, y, x = b // 16, (b // 4) % 4, b % 4
+        return (
+            ((z + 4 + sign * dz) % 4) * 16
+            + ((y + 4 + sign * dy) % 4) * 4
+            + (x + 4 + sign * dx) % 4
+        )
+
+    def message(it, turn, q):
         return pltpu.make_async_remote_copy(
-            src_ref=send.at[d],
-            dst_ref=recv.at[it, b],
+            src_ref=send.at[turn * G + q],
+            dst_ref=recv.at[it, turn * G + q],
             send_sem=send_sem,
-            recv_sem=recv_sem.at[it, i],
-            device_id=(other, d),
+            recv_sem=recv_sem.at[it, turn],
+            device_id=(other, partner(turn, q, 1)),
             device_id_type=MESH,
         )
 
@@ -214,17 +222,14 @@
         undo = make_table(u, tab, tab8, pick)
 
         def gather_group(turn, c):
-            i = far_first(turn)
-            dg = (mine + i) % groups
-            first = pl.multiple_of(dg * G, G)
-            if opening:
-                bases = base[pl.ds(first, G), :]
-                ws = [weight[q, pl.ds(first, G), :] for q in range(4)]
+            first = pl.multiple_of(turn * G, G)
             for q in range(G):
                 if opening:
-                    hot = one_hot(bases[q : q + 1])
+                    d = partner(turn, q, 1)
+                    at = base[pl.ds(d, 1), :]
+                    hot = one_hot(at)
                     hot, hot8 = hot.astype(bf16), hot.astype(f8)
-                    ps = patterns(bases[q : q + 1], [w[q : q + 1] for w in ws])
+                    ps = patterns(at, [weight[n, pl.ds(d, 1), :] for n in range(4)])
                     hots[first + q] = hot
                     hots8[first + q] = hot8
                     for o in range(3):
@@ -233,14 +238,17 @@
                     hot, hot8 = hots[first + q], hots8[first + q]
                     ps = [pats[first + q, o] for o in range(3)]
                 send[first + q] = interpolate(tab, tab8, hot, hot8, ps, undo)
-            if opening:
-
-                @pl.when(turn == 0)
-                def _():
-                    pl.semaphore_wait(barrier, blocks + 2)
-
-            for q in range(G):
-                message(it, i, first + (within + q) % G).start()
+                if q == 3:
+                    if opening:
+
+                        @pl.when(turn == 0)
+                        def _():
+                            pl.semaphore_wait(barrier, blocks + 2)
+
+                    for n in range(4):
+                        message(it, turn, n).start()
+            for n in range(4, G):
+                message(it, turn, n).start()
             return c
 
         lax.fori_loop(0, groups, gather_group, 0)
@@ -263,14 +271,16 @@
 
 
         def scatter_group(turn, c, half):
-            i = far_first(turn)
-            sg = (mine + groups - i) % groups
-            first = pl.multiple_of(sg * G, G)
+            first = pl.multiple_of(turn * G, G)
             if not half:
                 pltpu.make_async_copy(
-                    recv.at[it, pl.ds(first, G)], recv.at[it, pl.ds(first, G)], recv_sem.at[it, i]
+                    recv.at[it, pl.ds(first, G)],
+                    recv.at[it, pl.ds(first, G)],
+                    recv_sem.at[it, turn],
                 ).wait()
-            cells = cell[pl.ds(first, G), :]
+            cells = jnp.concatenate(
+                [cell[pl.ds(partner(turn, q, -1), 1), :] for q in range(G)], axis=0
+            )
             slots = pl.ds(pl.multiple_of(first * S, S), G * S)
             if opening and not half:
                 down_cells = jnp.transpose(cells.astype(f32)).astype(i32)

time: 97.5 us -> 102 us (1.046)
  Pallas kernels: 94.1 us -> 98.2 us
    pallas_call x1, Pallas kernels: 94.1 us -> 98.2 us  [on_device(): pl.pallas_call(functools.partial(kernel, blocks), out_shape=jax.ShapeDtyp...]
where the time goes in v6:
time: 102 us; the launch traced here: 99.9 us
  Pallas kernels  98.2 us (96%)
  local copies, waits for them, and re-layouts  1.72 us (2%)
    pallas_call x1, Pallas kernels, on_device(): pl.pallas_call(functools.partial(kernel, blocks), out_shape=jax.ShapeDtyp...  98.2 us

profile of v6, /device:TPU:32, one launch (start us, length us, event | category | flops | bytes accessed | tf_op | source)
XLA Modules:
  0.0 99.9 jit_solution(16552743989937176821)
XLA Ops:
  0.0 98.2 %shard_map.73 = f32[5,32,512]{2,1,0:T(8,128)} custom-call(f32[5,32,512]{2,1,0:T(8,128)} %bitcast.10, f32[5,32,512]{2,1,0:T(8,128)} %bitcast.11, f32[5,5,32,512]{3,2,1,0:T(8,128)} %bitcast.8, f32[4,32,512]{2,1,0:T(8,128)} %bitcast.12, s32[64,256]{1,0:T(8,128)} %bitcast.14, f32[4,64,256]{2,1,0:T(8,128)} %bitcast.13, s32[64,256]{1,0:T(8,128)} %bitcast.15), custom_call_target="tpu_custom_call" | custom-call | tf_op jit(solution)/shard_map/pallas_call | solution.py:505
  98.2 1.7 %copy.9 = f32[1,1,5,32,512]{4,3,2,1,0:T(8,128)} copy(f32[1,1,5,32,512]{4,3,2,1,0:T(8,128)} %bitcast.9) | data formatting | bytes 655360

commit v7 on v6

--- a/solution.py
+++ b/solution.py
@@ -238,16 +238,13 @@
                     hot, hot8 = hots[first + q], hots8[first + q]
                     ps = [pats[first + q, o] for o in range(3)]
                 send[first + q] = interpolate(tab, tab8, hot, hot8, ps, undo)
-                if q == 3:
-                    if opening:
-
-                        @pl.when(turn == 0)
-                        def _():
-                            pl.semaphore_wait(barrier, blocks + 2)
-
-                    for n in range(4):
-                        message(it, turn, n).start()
-            for n in range(4, G):
+            if opening:
+
+                @pl.when(turn == 0)
+                def _():
+                    pl.semaphore_wait(barrier, blocks + 2)
+
+            for n in range(G):
                 message(it, turn, n).start()
             return c
 

time: 102 us -> 98.2 us (0.963)
  the two profiles are of different devices: /device:TPU:32 before, /device:TPU:1 now
where the time goes in v7:
time: 98.2 us; the launch traced here: 98 us
  Pallas kernels  96.3 us (98%)
  local copies, waits for them, and re-layouts  1.72 us (2%)
    pallas_call x1, Pallas kernels, on_device(): pl.pallas_call(functools.partial(kernel, blocks), out_shape=jax.ShapeDtyp...  96.3 us

profile of v7, /device:TPU:1, one launch (start us, length us, event | category | flops | bytes accessed | tf_op | source)
XLA Modules:
  0.0 98.0 jit_solution(2273624059372998106)
XLA Ops:
  0.0 96.3 %shard_map.73 = f32[5,32,512]{2,1,0:T(8,128)} custom-call(f32[5,32,512]{2,1,0:T(8,128)} %bitcast.10, f32[5,32,512]{2,1,0:T(8,128)} %bitcast.11, f32[5,5,32,512]{3,2,1,0:T(8,128)} %bitcast.8, f32[4,32,512]{2,1,0:T(8,128)} %bitcast.12, s32[64,256]{1,0:T(8,128)} %bitcast.14, f32[4,64,256]{2,1,0:T(8,128)} %bitcast.13, s32[64,256]{1,0:T(8,128)} %bitcast.15), custom_call_target="tpu_custom_call" | custom-call | tf_op jit(solution)/shard_map/pallas_call | solution.py:502
  96.3 1.7 %copy.9 = f32[1,1,5,32,512]{4,3,2,1,0:T(8,128)} copy(f32[1,1,5,32,512]{4,3,2,1,0:T(8,128)} %bitcast.9) | data formatting | bytes 655360

commit v8 on v5

--- a/solution.py
+++ b/solution.py
@@ -213,7 +213,7 @@
     def sweep(it, opening):
         undo = make_table(u, tab, tab8, pick)
 
-        def gather_group(turn, c):
+        def gather_group(turn):
             i = far_first(turn)
             dg = (mine + i) % groups
             first = pl.multiple_of(dg * G, G)
@@ -233,17 +233,22 @@
                     hot, hot8 = hots[first + q], hots8[first + q]
                     ps = [pats[first + q, o] for o in range(3)]
                 send[first + q] = interpolate(tab, tab8, hot, hot8, ps, undo)
-            if opening:
-
-                @pl.when(turn == 0)
+            return i, first
+
+        def gather_two(n, c):
+            sent = [gather_group(2 * n), gather_group(2 * n + 1)]
+            if opening:
+
+                @pl.when(n == 0)
                 def _():
                     pl.semaphore_wait(barrier, blocks + 2)
 
-            for q in range(G):
-                message(it, i, first + (within + q) % G).start()
+            for i, first in sent:
+                for q in range(G):
+                    message(it, i, first + (within + q) % G).start()
             return c
 
-        lax.fori_loop(0, groups, gather_group, 0)
+        lax.fori_loop(0, groups // 2, gather_two, 0)
 
         if opening:
             for load in loads[3:]:
@@ -321,7 +326,16 @@
             acc[...] = jnp.zeros_like(acc)
             if opening:
                 marks[...] = jnp.zeros_like(marks)
-            lax.fori_loop(0, groups, functools.partial(scatter_group, half=half), 0)
+            if half:
+
+                def two_groups(n, c):
+                    scatter_group(2 * n, c, 1)
+                    scatter_group(2 * n + 1, c, 1)
+                    return c
+
+                lax.fori_loop(0, groups // 2, two_groups, 0)
+            else:
+                lax.fori_loop(0, groups, functools.partial(scatter_group, half=0), 0)
             placed = interleave(acc[0, :80, :], acc[0, 80:, :]) + interleave(acc[1, :80, :], acc[1, 80:, :])
             pieces = ((0, 8), (8, 16)) if half else ((0, 0), (8, 24))
             if opening:

time: 97.5 us -> 96.6 us (level)
  no operation moved by 1% of the time
where the time goes in v8:
time: 96.6 us; the launch traced here: 95.8 us
  Pallas kernels  94 us (97%)
  local copies, waits for them, and re-layouts  1.72 us (2%)
    pallas_call x1, Pallas kernels, on_device(): pl.pallas_call(functools.partial(kernel, blocks), out_shape=jax.ShapeDtyp...  94 us

profile of v8, /device:TPU:32, one launch (start us, length us, event | category | flops | bytes accessed | tf_op | source)
XLA Modules:
  0.0 95.8 jit_solution(2231355397554013007)
XLA Ops:
  0.0 94.0 %shard_map.73 = f32[5,32,512]{2,1,0:T(8,128)} custom-call(f32[5,32,512]{2,1,0:T(8,128)} %bitcast.10, f32[5,32,512]{2,1,0:T(8,128)} %bitcast.11, f32[5,5,32,512]{3,2,1,0:T(8,128)} %bitcast.8, f32[4,32,512]{2,1,0:T(8,128)} %bitcast.12, s32[64,256]{1,0:T(8,128)} %bitcast.14, f32[4,64,256]{2,1,0:T(8,128)} %bitcast.13, s32[64,256]{1,0:T(8,128)} %bitcast.15), custom_call_target="tpu_custom_call" | custom-call | tf_op jit(solution)/shard_map/pallas_call | solution.py:509
  94.0 1.7 %copy.9 = f32[1,1,5,32,512]{4,3,2,1,0:T(8,128)} copy(f32[1,1,5,32,512]{4,3,2,1,0:T(8,128)} %bitcast.9) | data formatting | bytes 655360
